TPU v7x, 32 devices: a whole 2x2x4 slice. The times are simulated.
32 devices in a mesh: groups: 2 (over x), paths: 16 (over z, y, core).
Axes of the slice: x: 2, y: 2, z: 4, core: 2. Of those that a mesh axis runs over, the one named last changes fastest.
Arguments:
- path_basis: bfloat16 [4096, 512], P(('groups', 'paths')), parts along dimension 0, may hold values from -6 to 6
- proxy_weight: bfloat16 [4096, 512], P(('groups', 'paths')), parts along dimension 0, may hold values from -0.25 to 0.25
- notional: bfloat16 [4096], P(('groups', 'paths')), parts along dimension 0, may hold values from -4 to 4
- set_of: int32 [4096], P('groups'), parts along dimension 0, may hold values from 0 to 511
- threshold_index: int32 [1024], P('groups'), parts along dimension 0, may hold values from 0 to 15
- threshold_levels: float32 [32], P('groups'), parts along dimension 0, may hold values from 0.5 to 20
- loss_rate: float32 [1024], P('groups'), parts along dimension 0, may hold values from 0.4 to 1
Outputs:
- expected_loss: float32 [2], P('groups'), parts along dimension 0
- basis_adjoint: float32 [4096, 512], P(('groups', 'paths')), parts along dimension 0
- weight_adjoint: float32 [4096, 512], P(('groups', 'paths')), parts along dimension 0
There are 2 independent parts, one for each index of `groups`. A program takes and returns all parts, laid end to end along the dimension named above; each array names one. Nothing has to cross between parts.
Inputs may be any that keep to these rules, and one draw needn't show every extreme that they name: `set_of`: netting set of each trade; set sizes are uneven.
All inputs are finite; a program needn't handle non-finite values.
Results may differ from a plain program's by a relative error of at most 0.0041.
Values may be sent and summed in bfloat16 or wider, within the bound.
No kernel may reach another device: no remote copies, remote signals or barrier semaphores. Data moves between devices by JAX's collectives and lax.ppermute only.
A program may use at most 64 MiB of HBM per device.

v0:
```python
import math

import jax
import jax.numpy as jnp
from jax import lax
from jax.sharding import PartitionSpec as P

REGRESSORS = 32


RIDGE_SCALE = 0.01
PRECISE = lax.Precision.HIGHEST


def table_rows(labels, classes, target_type):
    return (labels[:, None] == jnp.arange(classes, dtype=jnp.int32)[None, :]).astype(target_type)


def contract_rows(former, latter):
    return lax.dot_general(
        former,
        latter,
        (((0,), (0,)), ((), ())),
        precision=PRECISE,
        preferred_element_type=jnp.float32,
    )


def contract_cols(former, latter):
    return lax.dot_general(
        former,
        latter,
        (((1,), (1,)), ((), ())),
        precision=PRECISE,
        preferred_element_type=jnp.float32,
    )


def matrix_product(former, latter):
    return jnp.dot(former, latter, precision=PRECISE, preferred_element_type=jnp.float32)


def spd_solve(matrix, target):
    lower_factor = jnp.linalg.cholesky(matrix)
    halfway = lax.linalg.triangular_solve(lower_factor, target, left_side=True, lower=True)
    return lax.linalg.triangular_solve(
        lower_factor, halfway, left_side=True, lower=True, transpose_a=True
    )


def shards(
    path_basis, proxy_weight, notional, set_of, threshold_index, threshold_levels, loss_rate
):
    path_rows, feature_count = path_basis.shape
    paths_all = path_rows * lax.axis_size("paths")
    set_total = loss_rate.shape[0]
    design = jnp.concatenate(
        [
            jnp.ones((path_rows, 1), jnp.float32),
            path_basis[:, : REGRESSORS - 1].astype(jnp.float32),
        ],
        axis=1,
    )
    ridge_term = RIDGE_SCALE * paths_all * jnp.eye(REGRESSORS, dtype=jnp.float32)
    weight_all, notional_all = (
        lax.all_gather(proxy_weight, "paths", axis=0, tiled=True),
        lax.all_gather(notional, "paths", axis=0, tiled=True),
    )
    trade_count = weight_all.shape[0]
    block_cols = math.gcd(256, trade_count)
    block_count = trade_count // block_cols
    weight_blocks = weight_all.reshape(block_count, block_cols, feature_count)
    notional_blocks = notional_all.astype(jnp.float32).reshape(block_count, block_cols)
    set_blocks = set_of.reshape(block_count, block_cols)

    def forward_step(running, pieces):
        weight_block, notional_block, set_block = pieces
        pre_act = lax.dot_general(
            path_basis, weight_block, (((1,), (1,)), ((), ())), preferred_element_type=jnp.float32
        )
        trade_value = (notional_block[None, :] * jax.nn.softplus(pre_act)).astype(jnp.bfloat16)
        return (
            running
            + jnp.dot(
                trade_value,
                table_rows(set_block, set_total, jnp.bfloat16),
                preferred_element_type=jnp.float32,
            ),
            None,
        )

    exposure, _ = lax.scan(
        forward_step,
        jnp.zeros((path_rows, set_total), jnp.float32),
        (weight_blocks, notional_blocks, set_blocks),
    )
    thresholds = jnp.sum(
        table_rows(threshold_index, threshold_levels.shape[0], jnp.float32)
        * threshold_levels[None, :],
        axis=1,
    )
    set_columns = lax.all_to_all(exposure, "paths", split_axis=1, concat_axis=0, tiled=True)
    design_all = lax.all_gather(design, "paths", axis=0, tiled=True)
    local_sets = set_columns.shape[1]
    offset = lax.axis_index("paths") * local_sets
    thresh_here = lax.dynamic_slice_in_dim(thresholds, offset, local_sets)
    rate_here = lax.dynamic_slice_in_dim(loss_rate, offset, local_sets)
    gram_matrix = contract_rows(design_all, design_all) + ridge_term
    coeffs = spd_solve(gram_matrix, contract_rows(design_all, set_columns))
    fitted = matrix_product(design_all, coeffs)
    excess = fitted - thresh_here[None, :]
    seed_adjoint = rate_here[None, :] * jax.nn.sigmoid(excess)
    loss_sum = lax.psum(jnp.sum(rate_here[None, :] * jax.nn.softplus(excess)), "paths")
    solve_adjoint = spd_solve(gram_matrix, contract_rows(design_all, seed_adjoint))
    adjoint_full = matrix_product(design_all, solve_adjoint)
    exposure_adjoint = lax.all_to_all(
        adjoint_full.astype(jnp.bfloat16), "paths", split_axis=0, concat_axis=1, tiled=True
    )
    design_term = contract_cols(seed_adjoint - adjoint_full, coeffs) + contract_cols(
        set_columns - fitted, solve_adjoint
    )
    design_adjoint = lax.psum_scatter(design_term, "paths", scatter_dimension=0, tiled=True)
    expected_loss = (loss_sum / (paths_all * set_total)).reshape(1)

    def backward_step(running, pieces):
        weight_block, notional_block, set_block = pieces
        pre_trans = lax.dot_general(
            weight_block, path_basis, (((1,), (1,)), ((), ())), preferred_element_type=jnp.float32
        )
        spread_trans = lax.dot_general(
            table_rows(set_block, set_total, jnp.bfloat16),
            exposure_adjoint,
            (((1,), (1,)), ((), ())),
            preferred_element_type=jnp.float32,
        )
        slope_trans = (notional_block[:, None] * jax.nn.sigmoid(pre_trans) * spread_trans).astype(
            jnp.bfloat16
        )
        running = running + lax.dot_general(
            slope_trans, weight_block, (((0,), (0,)), ((), ())), preferred_element_type=jnp.float32
        )
        return (running, slope_trans)

    back_total, slope_stack = lax.scan(
        backward_step,
        jnp.zeros((path_rows, feature_count), jnp.float32),
        (weight_blocks, notional_blocks, set_blocks),
    )
    slopes = slope_stack.reshape(trade_count, path_rows)
    scale_factor = 1.0 / math.sqrt(paths_all)
    weight_adjoint = lax.psum_scatter(
        jnp.dot(slopes, path_basis, preferred_element_type=jnp.float32) * scale_factor,
        "paths",
        scatter_dimension=0,
        tiled=True,
    )
    padding = jnp.zeros((path_rows, feature_count - REGRESSORS + 1), jnp.float32)
    basis_adjoint = back_total + jnp.concatenate([design_adjoint[:, 1:], padding], axis=1)
    return (expected_loss, basis_adjoint, weight_adjoint)


def solution(mesh):
    placed = (
        P(("groups", "paths"), None),
        P(("groups", "paths"), None),
        P(("groups", "paths")),
        P("groups"),
        P("groups"),
        P("groups"),
        P("groups"),
    )
    return jax.shard_map(
        shards,
        mesh=mesh,
        in_specs=placed,
        out_specs=(P("groups"), P(("groups", "paths"), None), P(("groups", "paths"), None)),
        check_vma=False,
    )
```

profile of v0, /device:TPU:0, one launch (start us, length us, event | category | flops | bytes accessed | tf_op | source)
XLA Modules:
  0.0 244.3 jit_solution(9623423090362638424)
XLA Ops:
  8.6 23.1 %all-gather = bf16[16,1,128]{2,1,0:T(2,128)(2,1)S(1)} all-gather(bf16[1,1,128]{2,1,0:T(2,128)(2,1)} %bitcast.126), channel_id=1, replica_groups=mesh['groups'=2,'paths'=16] {'paths'}, dimensions={0}, use_global_device_ids=true | all-gather | bytes 4352 | tf_op jit(solution)/shard_map/all_gather | solution.py:67
  32.7 23.2 %all_gather.9 = f32[2048,32]{1,0:T(8,128)S(1)} all-gather(f32[128,32]{1,0:T(8,128)S(1)} %pad_convert_fusion), channel_id=1, replica_groups=mesh['groups'=2,'paths'=16] {'paths'}, dimensions={0}, use_global_device_ids=true | all-gather | bytes 278528 | tf_op jit(solution)/shard_map/all_gather | solution.py:103
  55.8 1.8 convolution_add_fusion.3
  57.8 12.6 %while.24 = (s32[]{:T(128)}, f32[128,512]{1,0:T(8,128)S(1)}, f32[8,256]{1,0:T(8,128)S(1)}, bf16[8,256,512]{2,1,0:T(8,128)(2,1)}, bf16[128,512]{1,0:T(8,128)(2,1)...) while((s32[]{:T(128)}, f32[128,512]{1,0:T(8,128)S(1)}, f32[8,256]{1,0:T(8,128)S(1)}, ...), condition=%wide.region_3.5_spmd.clone, body=%wide.region_2.4_spmd.clone.sunk | while | flops 67633152 | bytes 923763 | solution.py:92
  57.8 1.5 convolution_add_fusion.6
  59.4 1.5 convolution_add_fusion.6
  62.6 1.5 convolution_add_fusion.6
  64.1 1.5 convolution_add_fusion.6
  65.7 1.5 convolution_add_fusion.6
  67.3 1.5 convolution_add_fusion.6
  68.9 1.5 convolution_add_fusion.6
  71.2 5.4 %all-to-all-start = ((f32[128,16,32]{0,2,1:T(8,128)}), f32[128,16,32]{0,2,1:T(8,128)S(1)}, u32[]{:S(2)}, u32[]{:S(2)}) async-start(f32[128,16,32]{0,2,1:T(8,128)} %bitcast.7), calls=%async_computation | async-start | bytes 524288 | tf_op jit(solution)/shard_map/all_to_all | solution.py:102
  77.6 2.9 %cholesky.18 = f32[32,32]{1,0:T(8,128)S(1)} custom-call(f32[32,32]{1,0:T(8,128)S(1)} %fusion.45), custom_call_target="Cholesky" | custom-call | tf_op jit(solution)/shard_map/jit(cholesky)/cholesky | solution.py:44
  81.8 2.4 custom-call.13
  84.2 2.4 all-to-all-done
  86.7 1.8 fusion.30
  88.8 1.9 fusion.29
  90.7 1.8 fusion.46
  95.3 3.6 %all-to-all-start.1 = ((bf16[16,128,32]{1,2,0:T(8,128)(2,1)}), bf16[16,128,32]{1,2,0:T(8,128)(2,1)S(1)}, u32[]{:S(2)}, u32[]{:S(2)}) async-start(bf16[16,128,32]{1,2,0:T(8,128)(2,1)} %copy_bitcast_fusion), calls=%async_computation.1 | async-start | bytes 262144 | tf_op jit(solution)/shard_map/all_to_all | solution.py:116
  100.2 6.7 %all-to-all-done.1 = bf16[16,128,32]{1,2,0:T(8,128)(2,1)S(1)} async-done(((bf16[16,128,32]{1,2,0:T(8,128)(2,1)}), bf16[16,128,32]{1,2,0:T(8,128)(2,1)S(1)}, u32[]{:S(2)}, u32[]{:S(2)}) %all-to-all-start.1) | async-done | bytes 131104 | tf_op jit(solution)/shard_map/all_to_all | solution.py:116
  107.0 22.0 %while.25 = (s32[]{:T(128)}, f32[128,512]{1,0:T(8,128)S(1)}, bf16[8,256,128]{2,1,0:T(8,128)(2,1)S(1)}, f32[8,256]{1,0:T(8,128)S(1)}, bf16[8,256,512]{2,1,0:T(8,1...) while((s32[]{:T(128)}, f32[128,512]{1,0:T(8,128)S(1)}, ...), condition=%wide.region_8.12_spmd.clone, body=%wide.region_7.11_spmd.clone.sunk | while | flops 101122048 | bytes 1776771 | solution.py:144
  129.0 2.6 %convolution_multiply_fusion = f32[2048,512]{1,0:T(8,128)} fusion(bf16[2048,128]{1,0:T(8,128)(2,1)S(1)} %bitcast.120, bf16[128,512]{1,0:T(8,128)(2,1)S(1)} %get-tuple-element.356), kind=kOutput, calls=%fused_computation.35 | convolution fusion | flops 269484032 | bytes 4849664 | tf_op jit(solution)/shard_map/dot_general | solution.py:152
  131.7 30.9 %psum.7 = f32[]{:T(128)} all-reduce(f32[]{:T(128)} %get-tuple-element.198), channel_id=1, replica_groups=mesh['groups'=2,'paths'=16] {'paths'}, use_global_device_ids=true, to_apply=%region_6.10 | all-reduce | flops 1 | bytes 8 | tf_op jit(solution)/shard_map/psum | solution.py:113
  164.9 71.7 %reduce-scatter.5.cloned.1.call-done = f32[128,512]{1,0:T(8,128)} async-done(((f32[2048,512]{1,0:T(8,128)}), f32[128,512]{1,0:T(8,128)}) %reduce-scatter.5.cloned.1.call-update) | async-done | bytes 262160 | tf_op jit(solution)/shard_map/reduce_scatter | solution.py:151
  (101 shorter events, 35.0 us)
Async XLA Ops:
  7.2 50.6 %copy-start = (bf16[128,512]{1,0:T(8,128)(2,1)S(1)}, bf16[128,512]{1,0:T(8,128)(2,1)}, u32[]{:S(2)}) copy-start(bf16[128,512]{1,0:T(8,128)(2,1)} %param.16) | copy-start | bytes 393220
  7.2 50.6 %all-gather.3.cloned.1.call-start = ((), (), s32[]{:S(2)}) async-start(), calls=%async_computation.4 | async-start | bytes 2228224 | tf_op jit(solution)/shard_map/all_gather | solution.py:66
  57.8 18.8 %copy-start.1 = (s32[512]{0:T(512)S(1)}, s32[512]{0:T(512)}, u32[]{:S(2)}) copy-start(s32[512]{0:T(512)} %param.20) | copy-start | bytes 6148
  57.8 18.8 %copy-start.2 = (f32[16]{0:T(128)S(1)}, f32[16]{0:T(128)}, u32[]{:S(2)}) copy-start(f32[16]{0:T(128)} %param.21) | copy-start | bytes 196
  71.2 15.4 %all-to-all-start = ((f32[128,16,32]{0,2,1:T(8,128)}), f32[128,16,32]{0,2,1:T(8,128)S(1)}, u32[]{:S(2)}, u32[]{:S(2)}) async-start(f32[128,16,32]{0,2,1:T(8,128)} %bitcast.7), calls=%async_computation | async-start | bytes 524288 | tf_op jit(solution)/shard_map/all_to_all | solution.py:102
  95.3 11.6 %all-to-all-start.1 = ((bf16[16,128,32]{1,2,0:T(8,128)(2,1)}), bf16[16,128,32]{1,2,0:T(8,128)(2,1)S(1)}, u32[]{:S(2)}, u32[]{:S(2)}) async-start(bf16[16,128,32]{1,2,0:T(8,128)(2,1)} %copy_bitcast_fusion), calls=%async_computation.1 | async-start | bytes 262144 | tf_op jit(solution)/shard_map/all_to_all | solution.py:116
  99.0 64.4 %reduce-scatter.3.cloned.1.call-start = ((), (), s32[]{:S(2)}) async-start(), calls=%async_computation.5 | async-start | bytes 278528 | tf_op jit(solution)/shard_map/reduce_scatter | solution.py:122
  100.1 136.5 %reduce-scatter.5.cloned.1.call-start = ((), (), s32[]{:S(2)}) async-start(), calls=%async_computation.6 | async-start | bytes 4456448 | tf_op jit(solution)/shard_map/reduce_scatter | solution.py:151
Sparse Core Ops, SparseCore 0:
  10.2 45.8 all-gather.2
  103.9 56.7 reduce-scatter.2
  165.1 71.4 reduce-scatter.4
where the time goes:
time: 246 us; the launch traced here: 244 us
  waiting for transfers between devices  81.6 us (33%)
  blocking collectives  77.2 us (31%)
  matrix products  47.1 us (19%)
  between operations  15.7 us (6%)
  starting transfers between devices  9.12 us (4%)
  other arithmetic  7.58 us (3%)
  local copies, waits for them, and re-layouts  5.3 us (2%)
    reduce_scatter x1, waiting for transfers between devices, shards(): lax.psum_scatter(jnp.dot(slopes, path_basis, preferred_element_type=jnp.f...  71.7 us
    psum x1, blocking collectives, shards(): lax.psum(jnp.sum(rate_here[None, :] * jax.nn.softplus(excess)), 'paths')  30.9 us
    all_gather x1, blocking collectives, shards(): design_all = lax.all_gather(design, 'paths', axis=0, tiled=True)  23.2 us
    all_gather x1, blocking collectives, shards(): lax.all_gather(notional, 'paths', axis=0, tiled=True)  23.1 us
    dot_general x8, matrix products, forward_step(): jnp.dot(trade_value, table_rows(set_block, set_total, jnp.bfloat16), pref...  12.2 us
    dot_general x8, matrix products, backward_step(): lax.dot_general(weight_block, path_basis, (((1,), (1,)), ((), ())), prefe...  9.77 us
    dot_general x8, matrix products, backward_step(): lax.dot_general(slope_trans, weight_block, (((0,), (0,)), ((), ())), pref...  9.52 us
    all_to_all x1, waiting for transfers between devices, shards(): lax.all_to_all(adjoint_full.astype(jnp.bfloat16), 'paths', split_axis=0,...  6.75 us
  transfers between devices with their start and end apart: 5, of which 3 were waited for; matrix products, arithmetic and copies ran while one was open for 16% of the time, Pallas kernels for 0%

commit v1 on v0

v1 whole, which is shorter than its diff:
```python
import math

import jax
import jax.numpy as jnp
from jax import lax
from jax.sharding import PartitionSpec as P

REGRESSORS = 32
RIDGE_SCALE = 0.01
PRECISE = lax.Precision.HIGHEST
F32 = jnp.float32
BF16 = jnp.bfloat16


def split_axis(size):
    inner = max(d for d in range(1, math.isqrt(size) + 1) if size % d == 0)
    return size // inner, inner


def dot_dims(a, b, ca, cb, precision=None):
    return lax.dot_general(
        a, b, (((ca,), (cb,)), ((), ())), precision=precision, preferred_element_type=F32
    )


def one_hot(labels, classes, target_type):
    return (labels[:, None] == jnp.arange(classes, dtype=jnp.int32)[None, :]).astype(target_type)


def spd_solve(matrix, target):
    lower_factor = jnp.linalg.cholesky(matrix)
    halfway = lax.linalg.triangular_solve(lower_factor, target, left_side=True, lower=True)
    return lax.linalg.triangular_solve(
        lower_factor, halfway, left_side=True, lower=True, transpose_a=True
    )


def shards(
    path_basis, proxy_weight, notional, set_of, threshold_index, threshold_levels, loss_rate
):
    n = lax.axis_size("paths")
    outer, inner = split_axis(n)
    me = lax.axis_index("paths")
    my_outer, my_inner = me // inner, me % inner
    path_rows, features = path_basis.shape
    trade_rows = proxy_weight.shape[0]
    paths_all = path_rows * n
    sets = loss_rate.shape[0]
    quarter = sets // inner

    def along_inner(x, k):
        pairs = [(o * inner + i, o * inner + (i + k) % inner) for o in range(outer) for i in range(inner)]
        return lax.ppermute(x, "paths", pairs)

    def along_outer(x, k):
        pairs = [(o * inner + i, ((o + k) % outer) * inner + i) for o in range(outer) for i in range(inner)]
        return lax.ppermute(x, "paths", pairs)

    weight_slots = [proxy_weight] + [along_outer(proxy_weight, k) for k in range(1, outer)]
    basis_slots = [path_basis] + [along_inner(path_basis, k) for k in range(1, inner)]
    design = jnp.concatenate(
        [jnp.ones((1, path_rows), BF16), path_basis[:, : REGRESSORS - 1].T], axis=0
    )
    small = jnp.concatenate([design, jnp.pad(notional[None, :], ((0, 15), (0, max(path_rows, trade_rows) - trade_rows)))], axis=0)
    small_slots = [small] + [along_outer(small, k) for k in range(1, outer)]
    design_outer = jnp.stack([s[:REGRESSORS] for s in small_slots])
    design_slots = [design_outer] + [along_inner(design_outer, k) for k in range(1, inner)]
    design_all = jnp.stack(design_slots, axis=2).transpose(1, 0, 2, 3).reshape(REGRESSORS, paths_all)
    design_group = design_all[:, : inner * path_rows]

    weights = jnp.concatenate(weight_slots, axis=0)
    basis = jnp.concatenate(basis_slots, axis=0)
    notional_group = jnp.concatenate([s[REGRESSORS, :trade_rows] for s in small_slots]).astype(F32)
    set_blocks = set_of.reshape(n, trade_rows)
    set_group = jnp.concatenate(
        [
            lax.dynamic_index_in_dim(set_blocks, ((my_outer + outer - k) % outer) * inner + my_inner, 0, False)
            for k in range(outer)
        ]
    )
    in_set = one_hot(set_group, sets, BF16)

    pre_act = dot_dims(basis, weights, 1, 1)
    trade_value = (notional_group[None, :] * jax.nn.softplus(pre_act)).astype(BF16)
    slope = jax.nn.sigmoid(pre_act)
    trade_moment = dot_dims(design_group, trade_value, 1, 0)
    moment = dot_dims(trade_moment, in_set.astype(F32), 1, 0, PRECISE)

    def piece(x, size, axis, index):
        return lax.dynamic_slice_in_dim(x, index * size, size, axis)

    mine = piece(moment, quarter, 1, my_inner)
    for k in range(1, inner):
        mine = mine + along_inner(piece(moment, quarter, 1, (my_inner + k) % inner), k)
    part = mine
    for k in range(1, outer):
        mine = mine + along_outer(part, k)

    thresholds = jnp.sum(
        one_hot(threshold_index, threshold_levels.shape[0], F32) * threshold_levels[None, :], axis=1
    )
    thresh = piece(thresholds, quarter, 0, my_inner)
    rate = piece(loss_rate, quarter, 0, my_inner)
    design_wide = design_all.astype(F32)
    gram = dot_dims(design_all, design_all, 1, 1) + RIDGE_SCALE * paths_all * jnp.eye(
        REGRESSORS, dtype=F32
    )
    coeffs = spd_solve(gram, mine)
    fitted = dot_dims(design_wide, coeffs, 0, 0, PRECISE)
    excess = fitted - thresh[None, :]
    seed = rate[None, :] * jax.nn.sigmoid(excess)
    loss = jnp.sum(rate[None, :] * jax.nn.softplus(excess)) / (paths_all * sets)
    adjoint = spd_solve(gram, dot_dims(design_wide, seed, 1, 0, PRECISE))

    adjoint_slots = jnp.stack([adjoint] + [along_inner(adjoint, k) for k in range(1, inner)])
    order = (my_inner + inner - jnp.arange(inner)) % inner
    adjoint_all = adjoint_slots[order].transpose(1, 0, 2).reshape(REGRESSORS, sets)

    adjoint_trade = dot_dims(adjoint_all, in_set.astype(F32), 1, 1, PRECISE)
    spread = dot_dims(design_group.astype(F32), adjoint_trade, 0, 0, PRECISE).astype(BF16)
    trade_adjoint = (notional_group[None, :] * slope * spread.astype(F32)).astype(BF16)

    group_rows = inner * path_rows
    residual = seed[:group_rows] - dot_dims(design_group.astype(F32), adjoint, 0, 0, PRECISE)
    design_part = (
        dot_dims(coeffs, residual, 1, 1, PRECISE)
        - dot_dims(adjoint, fitted[:group_rows], 1, 1, PRECISE)
        + dot_dims(adjoint_trade, trade_value.astype(F32), 1, 1, PRECISE)
    )
    design_part = design_part.at[0].set(loss)

    weight_part = dot_dims(trade_adjoint, basis, 0, 0) * (1.0 / math.sqrt(paths_all))
    weight_total = weight_part[:trade_rows]
    for k in range(1, outer):
        sent = weight_part[k * trade_rows : (k + 1) * trade_rows].astype(BF16)
        weight_total = weight_total + along_outer(sent, outer - k).astype(F32)
    basis_part = dot_dims(trade_adjoint, weights, 1, 0)
    basis_total = basis_part[:path_rows]
    design_total = design_part[:, :path_rows]
    for k in range(1, inner):
        rows = slice(k * path_rows, (k + 1) * path_rows)
        basis_total = basis_total + along_inner(basis_part[rows].astype(BF16), inner - k).astype(F32)
        design_total = design_total + along_inner(design_part[:, rows], inner - k)
    basis_adjoint = basis_total + jnp.pad(
        design_total[1:].T, ((0, 0), (0, features - REGRESSORS + 1))
    )
    return (design_total[0, :1], basis_adjoint, weight_total)


def solution(mesh):
    placed = (
        P(("groups", "paths"), None),
        P(("groups", "paths"), None),
        P(("groups", "paths")),
        P("groups"),
        P("groups"),
        P("groups"),
        P("groups"),
    )
    return jax.shard_map(
        shards,
        mesh=mesh,
        in_specs=placed,
        out_specs=(P("groups"), P(("groups", "paths"), None), P(("groups", "paths"), None)),
        check_vma=False,
    )
```

time: 246 us -> 82.2 us (0.33)
  blocking collectives: 77.2 us -> 0 us
  waiting for transfers between devices: 81.6 us -> 19.4 us
  matrix products: 47.1 us -> 12.9 us
  starting transfers between devices: 9.12 us -> 32.2 us
  between operations: 15.7 us -> 1.82 us
    reduce_scatter x2 -> x0, waiting for transfers between devices: 71.7 us -> none  [the longest x1 71.7 us: shards(): lax.psum_scatter(jnp.dot(slopes, path_basis, preferred_element_type=jnp.f...]
    all_gather x2 -> x0, blocking collectives: 46.3 us -> none  [the longest x1 23.2 us: shards(): design_all = lax.all_gather(design, 'paths', axis=0, tiled=True)]
    dot_general x40 -> x14, matrix products: 46.4 us -> 12.2 us  [dot_dims(): lax.dot_general(a, b, (((ca,), (cb,)), ((), ())), precision=precision, pr...]
    ppermute x0 -> x30, starting transfers between devices: none -> 32.2 us  [the longest x12 18.4 us: along_outer(): return lax.ppermute(x, 'paths', pairs)]
    psum x1 -> x0, blocking collectives: 30.9 us -> none  [shards(): lax.psum(jnp.sum(rate_here[None, :] * jax.nn.softplus(excess)), 'paths')]
    ppermute x0 -> x30, waiting for transfers between devices: none -> 19.4 us  [the longest x12 13.5 us: along_outer(): return lax.ppermute(x, 'paths', pairs)]
    all_to_all x2 -> x0, waiting for transfers between devices: 9.17 us -> none  [the longest x1 6.75 us: shards(): lax.all_to_all(adjoint_full.astype(jnp.bfloat16), 'paths', split_axis=0,...]
    all_to_all x2 -> x0, starting transfers between devices: 9 us -> none  [the longest x1 5.37 us: shards(): lax.all_to_all(exposure, 'paths', split_axis=1, concat_axis=0, tiled=True)]
  transfers between devices with their start and end apart: 5 -> 30, of which waited for: 3 -> 12; matrix products, arithmetic and copies ran while one was open for 16% -> 14% of each run, Pallas kernels for 0% -> 0%
where the time goes in v1:
time: 82.2 us; the launch traced here: 81.7 us
  starting transfers between devices  32.2 us (39%)
  waiting for transfers between devices  19.4 us (24%)
  matrix products  12.9 us (16%)
  other arithmetic  7.76 us (9%)
  local copies, waits for them, and re-layouts  7.6 us (9%)
  between operations  1.82 us (2%)
    ppermute x12, starting transfers between devices, along_outer(): return lax.ppermute(x, 'paths', pairs)  18.4 us
    ppermute x18, starting transfers between devices, along_inner(): return lax.ppermute(x, 'paths', pairs)  13.8 us
    ppermute x12, waiting for transfers between devices, along_outer(): return lax.ppermute(x, 'paths', pairs)  13.5 us
    dot_general x14, matrix products, dot_dims(): lax.dot_general(a, b, (((ca,), (cb,)), ((), ())), precision=precision, pr...  12.2 us
    ppermute x18, waiting for transfers between devices, along_inner(): return lax.ppermute(x, 'paths', pairs)  5.97 us
    another operation x3, other arithmetic, spd_solve(): lower_factor = jnp.linalg.cholesky(matrix)  3.59 us
    another operation x2, other arithmetic, spd_solve(): lax.linalg.triangular_solve(lower_factor, halfway, left_side=True, lower=...  3.09 us
    unnamed x22, local copies, waits for them, and re-layouts  3.07 us
  transfers between devices with their start and end apart: 30, of which 12 were waited for; matrix products, arithmetic and copies ran while one was open for 14% of the time, Pallas kernels for 0%

profile of v1, /device:TPU:0, one launch (start us, length us, event | category | flops | bytes accessed | tf_op | source)
XLA Modules:
  0.0 81.7 jit_solution(6209358880318661583)
XLA Ops:
  1.6 5.1 %collective-permute-start.2 = (bf16[48,128]{1,0:T(8,128)(2,1)S(1)}, bf16[48,128]{1,0:T(8,128)(2,1)S(1)}, u32[]{:S(2)}, u32[]{:S(2)}) collective-permute-start(bf16[48,128]{1,0:T(8,128)(2,1)S(1)} %fusion.41), channel_id=1, source_target_pairs={{0,12},{1,13},{2,14},{3,15},{4,0},{5,1},{6,2},{7,3},{8,4},{9,5},{1... | collective-permute-start | bytes 36872 | tf_op jit(solution)/shard_map/ppermute | solution.py:57
  7.6 1.6 %collective-permute-start.7 = (bf16[128,512]{1,0:T(8,128)(2,1)}, bf16[128,512]{1,0:T(8,128)(2,1)S(1)}, u32[]{:S(2)}, u32[]{:S(2)}) collective-permute-start(bf16[128,512]{1,0:T(8,128)(2,1)} %param.14), channel_id=1, source_target_pairs={{0,2},{1,3},{2,0},{3,1},{4,6},{5,7},{6,4},{7,5},{8,10},{9,11},{10,... | collective-permute-start | bytes 393224 | tf_op jit(solution)/shard_map/ppermute | solution.py:53
  12.7 1.5 %collective-permute-start.5 = (bf16[4,32,128]{2,1,0:T(8,128)(2,1)S(1)}, bf16[4,32,128]{2,1,0:T(8,128)(2,1)S(1)}, u32[]{:S(2)}, u32[]{:S(2)}) collective-permute-start(bf16[4,32,128]{2,1,0:T(8,128)(2,1)S(1)} %get-tuple-element.42), channel_id=1, source_target_pairs={{0,3},{1,0},{2,1},{3,2},{4,7},{5,4},{6,5},{7,6},{8,11},{9,8},{10,9... | collective-permute-start | bytes 98312 | tf_op jit(solution)/shard_map/ppermute | solution.py:53
  15.8 1.7 %collective-permute-start.8 = (bf16[128,512]{1,0:T(8,128)(2,1)S(1)}, bf16[128,512]{1,0:T(8,128)(2,1)S(1)}, u32[]{:S(2)}, u32[]{:S(2)}) collective-permute-start(bf16[128,512]{1,0:T(8,128)(2,1)S(1)} %copy-done.2), channel_id=1, source_target_pairs={{0,3},{1,0},{2,1},{3,2},{4,7},{5,4},{6,5},{7,6},{8,11},{9,8},{10,9... | collective-permute-start | bytes 393224 | tf_op jit(solution)/shard_map/ppermute | solution.py:53
  18.4 2.5 %collective-permute-start.9 = (bf16[128,512]{1,0:T(8,128)(2,1)S(1)}, bf16[128,512]{1,0:T(8,128)(2,1)S(1)}, u32[]{:S(2)}, u32[]{:S(2)}) collective-permute-start(bf16[128,512]{1,0:T(8,128)(2,1)S(1)} %copy-done.3), channel_id=1, source_target_pairs={{0,4},{1,5},{2,6},{3,7},{4,8},{5,9},{6,10},{7,11},{8,12},{9,13},{1... | collective-permute-start | bytes 393224 | tf_op jit(solution)/shard_map/ppermute | solution.py:57
  22.0 2.9 %cholesky.18 = f32[32,32]{1,0:T(8,128)S(1)} custom-call(f32[32,32]{1,0:T(8,128)S(1)} %fusion.37), custom_call_target="Cholesky" | custom-call | tf_op jit(solution)/shard_map/jit(cholesky)/cholesky | solution.py:31
  25.1 1.5 %collective-permute-start.11 = (bf16[128,512]{1,0:T(8,128)(2,1)S(1)}, bf16[128,512]{1,0:T(8,128)(2,1)S(1)}, u32[]{:S(2)}, u32[]{:S(2)}) collective-permute-start(bf16[128,512]{1,0:T(8,128)(2,1)S(1)} %copy-done.3), channel_id=1, source_target_pairs={{0,12},{1,13},{2,14},{3,15},{4,0},{5,1},{6,2},{7,3},{8,4},{9,5},{1... | collective-permute-start | bytes 393224 | tf_op jit(solution)/shard_map/ppermute | solution.py:57
  26.8 3.2 %collective-permute-done.10 = bf16[128,512]{1,0:T(8,128)(2,1)S(1)} collective-permute-done((bf16[128,512]{1,0:T(8,128)(2,1)S(1)}, bf16[128,512]{1,0:T(8,128)(2,1)S(1)}, u32[]{:S(2)}, u32[]{:S(2)}) %collective-permute-start.10) | collective-permute-done | bytes 131104 | tf_op jit(solution)/shard_map/ppermute | solution.py:57
  30.8 1.8 %fusion.6 = (bf16[512,512]{1,0:T(8,128)(2,1)S(1)}, f32[512,512]{1,0:T(8,128)}) fusion(f32[512]{0:T(512)S(1)} %maximum_convert_fusion, bf16[512,512]{1,0:T(8,128)(2,1)S(1)} %constant_dynamic-update-slice_fusion, bf16[512,512]{1,0:T(8,128)(2,1)S(1)} %constant_dynamic-update-slice_fusion.4), kind=kOutput, calls=%fused_computation.14 | convolution fusion | flops 270532608 | bytes 2623488 | tf_op jit(solution)/shard_map/dot_general | solution.py:21
  33.4 1.6 %collective-permute-start.13 = (f32[32,128]{1,0:T(8,128)S(1)}, f32[32,128]{1,0:T(8,128)S(1)}, u32[]{:S(2)}, u32[]{:S(2)}) collective-permute-start(f32[32,128]{1,0:T(8,128)S(1)} %get-tuple-element.40), channel_id=1, source_target_pairs={{0,2},{1,3},{2,0},{3,1},{4,6},{5,7},{6,4},{7,5},{8,10},{9,11},{10,... | collective-permute-start | bytes 49160 | tf_op jit(solution)/shard_map/ppermute | solution.py:53
  35.8 1.4 %collective-permute-done.13 = f32[32,128]{1,0:T(8,128)S(1)} collective-permute-done((f32[32,128]{1,0:T(8,128)S(1)}, f32[32,128]{1,0:T(8,128)S(1)}, u32[]{:S(2)}, u32[]{:S(2)}) %collective-permute-start.13) | collective-permute-done | bytes 16416 | tf_op jit(solution)/shard_map/ppermute | solution.py:53
  38.2 2.6 %collective-permute-start.17 = (f32[32,128]{1,0:T(8,128)S(1)}, f32[32,128]{1,0:T(8,128)S(1)}, u32[]{:S(2)}, u32[]{:S(2)}) collective-permute-start(f32[32,128]{1,0:T(8,128)S(1)} %add_add_fusion), channel_id=1, source_target_pairs={{0,12},{1,13},{2,14},{3,15},{4,0},{5,1},{6,2},{7,3},{8,4},{9,5},{1... | collective-permute-start | bytes 49160 | tf_op jit(solution)/shard_map/ppermute | solution.py:57
  42.4 2.4 %custom-call.11 = f32[1,32,32]{1,2,0:T(8,128)S(1)} custom-call(f32[1,32,32]{2,1,0:T(8,128)S(1)} %fusion.26), custom_call_target="InvertDiagBlocksLowerTriangular" | custom-call | tf_op jit(solution)/shard_map/triangular_solve/custom-call.2 | solution.py:33
  45.5 1.8 %collective-permute-done.15 = f32[32,128]{1,0:T(8,128)S(1)} collective-permute-done((f32[32,128]{1,0:T(8,128)S(1)}, f32[32,128]{1,0:T(8,128)S(1)}, u32[]{:S(2)}, u32[]{:S(2)}) %collective-permute-start.15) | collective-permute-done | bytes 16416 | tf_op jit(solution)/shard_map/ppermute | solution.py:57
  47.6 2.9 %fusion.8 = (f32[]{:T(128)}, f32[2048,128]{1,0:T(8,128)S(1)}, f32[2048,128]{1,0:T(8,128)}) fusion(f32[128]{0:T(128)S(1)} %dynamic_slice.40, f32[128]{0:T(128)S(1)} %dynamic_slice.39, bf16[32,2048]{1,0:T(8,128)(2,1)S(1)} %reshape.138, f32[32,128]{1,0:T(8,128)S(1)} %fusion.35), kind=kOutput, calls=%fused_computation.16 | convolution fusion | flops 104071168 | bytes 2245636 | tf_op jit(solution)/shard_map/dot_general | solution.py:21
  51.4 1.4 %collective-permute-start.19 = (f32[32,128]{1,0:T(8,128)S(1)}, f32[32,128]{1,0:T(8,128)S(1)}, u32[]{:S(2)}, u32[]{:S(2)}) collective-permute-start(f32[32,128]{1,0:T(8,128)S(1)} %fusion.31), channel_id=1, source_target_pairs={{0,2},{1,3},{2,0},{3,1},{4,6},{5,7},{6,4},{7,5},{8,10},{9,11},{10,... | collective-permute-start | bytes 49160 | tf_op jit(solution)/shard_map/ppermute | solution.py:53
  57.9 2.0 %fusion.2 = bf16[512,512]{1,0:T(8,128)(2,1)S(1)} fusion(f32[32,512]{1,0:T(8,128)S(1)} %fusion.9, f32[512,512]{1,0:T(8,128)} %get-tuple-element.48, f32[512]{0:T(512)S(1)} %maximum_convert_fusion, bf16[32,2048]{1,0:T(8,128)(2,1)S(1)} %reshape.138), kind=kOutput, calls=%fused_computation.7 | convolution fusion | flops 102760448 | bytes 1673216 | tf_op jit(solution)/shard_map/dot_general | solution.py:21
  63.7 1.4 %collective-permute-start.21 = (f32[32,128]{1,0:T(8,128)S(1)}, f32[32,128]{1,0:T(8,128)S(1)}, u32[]{:S(2)}, u32[]{:S(2)}) collective-permute-start(f32[32,128]{1,0:T(8,128)S(1)} %get-tuple-element.35), channel_id=1, source_target_pairs={{0,3},{1,0},{2,1},{3,2},{4,7},{5,4},{6,5},{7,6},{8,11},{9,8},{10,9... | collective-permute-start | bytes 49160 | tf_op jit(solution)/shard_map/ppermute | solution.py:53
  65.2 1.3 %collective-permute-start.25 = (bf16[128,512]{0,1:T(8,128)(2,1)S(1)}, bf16[128,512]{0,1:T(8,128)(2,1)S(1)}, u32[]{:S(2)}, u32[]{:S(2)}) collective-permute-start(bf16[128,512]{0,1:T(8,128)(2,1)S(1)} %get-tuple-element.34), channel_id=1, source_target_pairs={{0,2},{1,3},{2,0},{3,1},{4,6},{5,7},{6,4},{7,5},{8,10},{9,11},{10,... | collective-permute-start | bytes 393224 | tf_op jit(solution)/shard_map/ppermute | solution.py:53
  67.2 1.4 %collective-permute-start.24 = (bf16[128,512]{0,1:T(8,128)(2,1)S(1)}, bf16[128,512]{0,1:T(8,128)(2,1)S(1)}, u32[]{:S(2)}, u32[]{:S(2)}) collective-permute-start(bf16[128,512]{0,1:T(8,128)(2,1)S(1)} %get-tuple-element.32), channel_id=1, source_target_pairs={{0,3},{1,0},{2,1},{3,2},{4,7},{5,4},{6,5},{7,6},{8,11},{9,8},{10,9... | collective-permute-start | bytes 393224 | tf_op jit(solution)/shard_map/ppermute | solution.py:53
  68.6 2.0 %collective-permute-start.28 = (bf16[128,512]{1,0:T(8,128)(2,1)S(1)}, bf16[128,512]{1,0:T(8,128)(2,1)S(1)}, u32[]{:S(2)}, u32[]{:S(2)}) collective-permute-start(bf16[128,512]{1,0:T(8,128)(2,1)S(1)} %get-tuple-element.31), channel_id=1, source_target_pairs={{0,8},{1,9},{2,10},{3,11},{4,12},{5,13},{6,14},{7,15},{8,0},{9,1},... | collective-permute-start | bytes 393224 | tf_op jit(solution)/shard_map/ppermute | solution.py:57
  71.1 1.9 %collective-permute-start.27 = (bf16[128,512]{1,0:T(8,128)(2,1)S(1)}, bf16[128,512]{1,0:T(8,128)(2,1)S(1)}, u32[]{:S(2)}, u32[]{:S(2)}) collective-permute-start(bf16[128,512]{1,0:T(8,128)(2,1)S(1)} %get-tuple-element.29), channel_id=1, source_target_pairs={{0,12},{1,13},{2,14},{3,15},{4,0},{5,1},{6,2},{7,3},{8,4},{9,5},{1... | collective-permute-start | bytes 393224 | tf_op jit(solution)/shard_map/ppermute | solution.py:57
  73.9 3.2 %collective-permute-done.29 = bf16[128,512]{1,0:T(8,128)(2,1)S(1)} collective-permute-done((bf16[128,512]{1,0:T(8,128)(2,1)}, bf16[128,512]{1,0:T(8,128)(2,1)S(1)}, u32[]{:S(2)}, u32[]{:S(2)}) %collective-permute-start.29) | collective-permute-done | bytes 131104 | tf_op jit(solution)/shard_map/ppermute | solution.py:57
  77.1 3.9 %collective-permute-done.28 = bf16[128,512]{1,0:T(8,128)(2,1)S(1)} collective-permute-done((bf16[128,512]{1,0:T(8,128)(2,1)S(1)}, bf16[128,512]{1,0:T(8,128)(2,1)S(1)}, u32[]{:S(2)}, u32[]{:S(2)}) %collective-permute-start.28) | collective-permute-done | bytes 131104 | tf_op jit(solution)/shard_map/ppermute | solution.py:57
  (122 shorter events, 26.9 us)
Async XLA Ops:
  1.6 11.1 %collective-permute-start.2 = (bf16[48,128]{1,0:T(8,128)(2,1)S(1)}, bf16[48,128]{1,0:T(8,128)(2,1)S(1)}, u32[]{:S(2)}, u32[]{:S(2)}) collective-permute-start(bf16[48,128]{1,0:T(8,128)(2,1)S(1)} %fusion.41), channel_id=1, source_target_pairs={{0,12},{1,13},{2,14},{3,15},{4,0},{5,1},{6,2},{7,3},{8,4},{9,5},{1... | collective-permute-start | bytes 36872 | tf_op jit(solution)/shard_map/ppermute | solution.py:57
  6.6 6.0 %collective-permute-start.1 = (bf16[48,128]{1,0:T(8,128)(2,1)S(1)}, bf16[48,128]{1,0:T(8,128)(2,1)S(1)}, u32[]{:S(2)}, u32[]{:S(2)}) collective-permute-start(bf16[48,128]{1,0:T(8,128)(2,1)S(1)} %fusion.41), channel_id=1, source_target_pairs={{0,8},{1,9},{2,10},{3,11},{4,12},{5,13},{6,14},{7,15},{8,0},{9,1},... | collective-permute-start | bytes 36872 | tf_op jit(solution)/shard_map/ppermute | solution.py:57
  6.6 6.0 %collective-permute-start = (bf16[48,128]{1,0:T(8,128)(2,1)S(1)}, bf16[48,128]{1,0:T(8,128)(2,1)S(1)}, u32[]{:S(2)}, u32[]{:S(2)}) collective-permute-start(bf16[48,128]{1,0:T(8,128)(2,1)S(1)} %fusion.41), channel_id=1, source_target_pairs={{0,4},{1,5},{2,6},{3,7},{4,8},{5,9},{6,10},{7,11},{8,12},{9,13},{1... | collective-permute-start | bytes 36872 | tf_op jit(solution)/shard_map/ppermute | solution.py:57
  7.6 17.5 %collective-permute-start.6 = (bf16[128,512]{1,0:T(8,128)(2,1)}, bf16[128,512]{1,0:T(8,128)(2,1)S(1)}, u32[]{:S(2)}, u32[]{:S(2)}) collective-permute-start(bf16[128,512]{1,0:T(8,128)(2,1)} %param.14), channel_id=1, source_target_pairs={{0,1},{1,2},{2,3},{3,0},{4,5},{5,6},{6,7},{7,4},{8,9},{9,10},{10,1... | collective-permute-start | bytes 393224 | tf_op jit(solution)/shard_map/ppermute | solution.py:53
  7.6 19.0 %collective-permute-start.7 = (bf16[128,512]{1,0:T(8,128)(2,1)}, bf16[128,512]{1,0:T(8,128)(2,1)S(1)}, u32[]{:S(2)}, u32[]{:S(2)}) collective-permute-start(bf16[128,512]{1,0:T(8,128)(2,1)} %param.14), channel_id=1, source_target_pairs={{0,2},{1,3},{2,0},{3,1},{4,6},{5,7},{6,4},{7,5},{8,10},{9,11},{10,... | collective-permute-start | bytes 393224 | tf_op jit(solution)/shard_map/ppermute | solution.py:53
  14.2 4.2 %collective-permute-start.4 = (bf16[4,32,128]{2,1,0:T(8,128)(2,1)S(1)}, bf16[4,32,128]{2,1,0:T(8,128)(2,1)S(1)}, u32[]{:S(2)}, u32[]{:S(2)}) collective-permute-start(bf16[4,32,128]{2,1,0:T(8,128)(2,1)S(1)} %get-tuple-element.42), channel_id=1, source_target_pairs={{0,2},{1,3},{2,0},{3,1},{4,6},{5,7},{6,4},{7,5},{8,10},{9,11},{10,... | collective-permute-start | bytes 98312 | tf_op jit(solution)/shard_map/ppermute | solution.py:53
  14.7 6.2 %collective-permute-start.3 = (bf16[4,32,128]{2,1,0:T(8,128)(2,1)S(1)}, bf16[4,32,128]{2,1,0:T(8,128)(2,1)S(1)}, u32[]{:S(2)}, u32[]{:S(2)}) collective-permute-start(bf16[4,32,128]{2,1,0:T(8,128)(2,1)S(1)} %get-tuple-element.42), channel_id=1, source_target_pairs={{0,1},{1,2},{2,3},{3,0},{4,5},{5,6},{6,7},{7,4},{8,9},{9,10},{10,1... | collective-permute-start | bytes 98312 | tf_op jit(solution)/shard_map/ppermute | solution.py:53
  15.8 10.9 %collective-permute-start.8 = (bf16[128,512]{1,0:T(8,128)(2,1)S(1)}, bf16[128,512]{1,0:T(8,128)(2,1)S(1)}, u32[]{:S(2)}, u32[]{:S(2)}) collective-permute-start(bf16[128,512]{1,0:T(8,128)(2,1)S(1)} %copy-done.2), channel_id=1, source_target_pairs={{0,3},{1,0},{2,1},{3,2},{4,7},{5,4},{6,5},{7,6},{8,11},{9,8},{10,9... | collective-permute-start | bytes 393224 | tf_op jit(solution)/shard_map/ppermute | solution.py:53
  18.4 8.4 %collective-permute-start.9 = (bf16[128,512]{1,0:T(8,128)(2,1)S(1)}, bf16[128,512]{1,0:T(8,128)(2,1)S(1)}, u32[]{:S(2)}, u32[]{:S(2)}) collective-permute-start(bf16[128,512]{1,0:T(8,128)(2,1)S(1)} %copy-done.3), channel_id=1, source_target_pairs={{0,4},{1,5},{2,6},{3,7},{4,8},{5,9},{6,10},{7,11},{8,12},{9,13},{1... | collective-permute-start | bytes 393224 | tf_op jit(solution)/shard_map/ppermute | solution.py:57
  20.8 9.1 %collective-permute-start.10 = (bf16[128,512]{1,0:T(8,128)(2,1)S(1)}, bf16[128,512]{1,0:T(8,128)(2,1)S(1)}, u32[]{:S(2)}, u32[]{:S(2)}) collective-permute-start(bf16[128,512]{1,0:T(8,128)(2,1)S(1)} %copy-done.3), channel_id=1, source_target_pairs={{0,8},{1,9},{2,10},{3,11},{4,12},{5,13},{6,14},{7,15},{8,0},{9,1},... | collective-permute-start | bytes 393224 | tf_op jit(solution)/shard_map/ppermute | solution.py:57
  25.1 5.6 %collective-permute-start.11 = (bf16[128,512]{1,0:T(8,128)(2,1)S(1)}, bf16[128,512]{1,0:T(8,128)(2,1)S(1)}, u32[]{:S(2)}, u32[]{:S(2)}) collective-permute-start(bf16[128,512]{1,0:T(8,128)(2,1)S(1)} %copy-done.3), channel_id=1, source_target_pairs={{0,12},{1,13},{2,14},{3,15},{4,0},{5,1},{6,2},{7,3},{8,4},{9,5},{1... | collective-permute-start | bytes 393224 | tf_op jit(solution)/shard_map/ppermute | solution.py:57
  33.4 3.8 %collective-permute-start.13 = (f32[32,128]{1,0:T(8,128)S(1)}, f32[32,128]{1,0:T(8,128)S(1)}, u32[]{:S(2)}, u32[]{:S(2)}) collective-permute-start(f32[32,128]{1,0:T(8,128)S(1)} %get-tuple-element.40), channel_id=1, source_target_pairs={{0,2},{1,3},{2,0},{3,1},{4,6},{5,7},{6,4},{7,5},{8,10},{9,11},{10,... | collective-permute-start | bytes 49160 | tf_op jit(solution)/shard_map/ppermute | solution.py:53
  38.2 6.7 %collective-permute-start.17 = (f32[32,128]{1,0:T(8,128)S(1)}, f32[32,128]{1,0:T(8,128)S(1)}, u32[]{:S(2)}, u32[]{:S(2)}) collective-permute-start(f32[32,128]{1,0:T(8,128)S(1)} %add_add_fusion), channel_id=1, source_target_pairs={{0,12},{1,13},{2,14},{3,15},{4,0},{5,1},{6,2},{7,3},{8,4},{9,5},{1... | collective-permute-start | bytes 49160 | tf_op jit(solution)/shard_map/ppermute | solution.py:57
  40.8 4.6 %collective-permute-start.16 = (f32[32,128]{1,0:T(8,128)S(1)}, f32[32,128]{1,0:T(8,128)S(1)}, u32[]{:S(2)}, u32[]{:S(2)}) collective-permute-start(f32[32,128]{1,0:T(8,128)S(1)} %add_add_fusion), channel_id=1, source_target_pairs={{0,8},{1,9},{2,10},{3,11},{4,12},{5,13},{6,14},{7,15},{8,0},{9,1},... | collective-permute-start | bytes 49160 | tf_op jit(solution)/shard_map/ppermute | solution.py:57
  41.7 5.5 %collective-permute-start.15 = (f32[32,128]{1,0:T(8,128)S(1)}, f32[32,128]{1,0:T(8,128)S(1)}, u32[]{:S(2)}, u32[]{:S(2)}) collective-permute-start(f32[32,128]{1,0:T(8,128)S(1)} %add_add_fusion), channel_id=1, source_target_pairs={{0,4},{1,5},{2,6},{3,7},{4,8},{5,9},{6,10},{7,11},{8,12},{9,13},{1... | collective-permute-start | bytes 49160 | tf_op jit(solution)/shard_map/ppermute | solution.py:57
  62.8 4.4 %collective-permute-start.23 = (f32[32,128]{1,0:T(8,128)S(1)}, f32[32,128]{1,0:T(8,128)S(1)}, u32[]{:S(2)}, u32[]{:S(2)}) collective-permute-start(f32[32,128]{1,0:T(8,128)S(1)} %get-tuple-element.36), channel_id=1, source_target_pairs={{0,1},{1,2},{2,3},{3,0},{4,5},{5,6},{6,7},{7,4},{8,9},{9,10},{10,1... | collective-permute-start | bytes 49160 | tf_op jit(solution)/shard_map/ppermute | solution.py:53
  62.8 5.8 %collective-permute-start.22 = (f32[32,128]{1,0:T(8,128)S(1)}, f32[32,128]{1,0:T(8,128)S(1)}, u32[]{:S(2)}, u32[]{:S(2)}) collective-permute-start(f32[32,128]{1,0:T(8,128)S(1)} %get-tuple-element.37), channel_id=1, source_target_pairs={{0,2},{1,3},{2,0},{3,1},{4,6},{5,7},{6,4},{7,5},{8,10},{9,11},{10,... | collective-permute-start | bytes 49160 | tf_op jit(solution)/shard_map/ppermute | solution.py:53
  63.7 5.0 %collective-permute-start.21 = (f32[32,128]{1,0:T(8,128)S(1)}, f32[32,128]{1,0:T(8,128)S(1)}, u32[]{:S(2)}, u32[]{:S(2)}) collective-permute-start(f32[32,128]{1,0:T(8,128)S(1)} %get-tuple-element.35), channel_id=1, source_target_pairs={{0,3},{1,0},{2,1},{3,2},{4,7},{5,4},{6,5},{7,6},{8,11},{9,8},{10,9... | collective-permute-start | bytes 49160 | tf_op jit(solution)/shard_map/ppermute | solution.py:53
  65.1 6.0 %collective-permute-start.26 = (bf16[128,512]{0,1:T(8,128)(2,1)S(1)}, bf16[128,512]{0,1:T(8,128)(2,1)S(1)}, u32[]{:S(2)}, u32[]{:S(2)}) collective-permute-start(bf16[128,512]{0,1:T(8,128)(2,1)S(1)} %get-tuple-element.33), channel_id=1, source_target_pairs={{0,1},{1,2},{2,3},{3,0},{4,5},{5,6},{6,7},{7,4},{8,9},{9,10},{10,1... | collective-permute-start | bytes 393224 | tf_op jit(solution)/shard_map/ppermute | solution.py:53
  65.2 7.8 %collective-permute-start.25 = (bf16[128,512]{0,1:T(8,128)(2,1)S(1)}, bf16[128,512]{0,1:T(8,128)(2,1)S(1)}, u32[]{:S(2)}, u32[]{:S(2)}) collective-permute-start(bf16[128,512]{0,1:T(8,128)(2,1)S(1)} %get-tuple-element.34), channel_id=1, source_target_pairs={{0,2},{1,3},{2,0},{3,1},{4,6},{5,7},{6,4},{7,5},{8,10},{9,11},{10,... | collective-permute-start | bytes 393224 | tf_op jit(solution)/shard_map/ppermute | solution.py:53
  67.2 5.8 %collective-permute-start.24 = (bf16[128,512]{0,1:T(8,128)(2,1)S(1)}, bf16[128,512]{0,1:T(8,128)(2,1)S(1)}, u32[]{:S(2)}, u32[]{:S(2)}) collective-permute-start(bf16[128,512]{0,1:T(8,128)(2,1)S(1)} %get-tuple-element.32), channel_id=1, source_target_pairs={{0,3},{1,0},{2,1},{3,2},{4,7},{5,4},{6,5},{7,6},{8,11},{9,8},{10,9... | collective-permute-start | bytes 393224 | tf_op jit(solution)/shard_map/ppermute | solution.py:53
  68.6 8.5 %collective-permute-start.29 = (bf16[128,512]{1,0:T(8,128)(2,1)}, bf16[128,512]{1,0:T(8,128)(2,1)S(1)}, u32[]{:S(2)}, u32[]{:S(2)}) collective-permute-start(bf16[128,512]{1,0:T(8,128)(2,1)} %get-tuple-element.30), channel_id=1, source_target_pairs={{0,4},{1,5},{2,6},{3,7},{4,8},{5,9},{6,10},{7,11},{8,12},{9,13},{1... | collective-permute-start | bytes 393224 | tf_op jit(solution)/shard_map/ppermute | solution.py:57
  68.6 12.4 %collective-permute-start.28 = (bf16[128,512]{1,0:T(8,128)(2,1)S(1)}, bf16[128,512]{1,0:T(8,128)(2,1)S(1)}, u32[]{:S(2)}, u32[]{:S(2)}) collective-permute-start(bf16[128,512]{1,0:T(8,128)(2,1)S(1)} %get-tuple-element.31), channel_id=1, source_target_pairs={{0,8},{1,9},{2,10},{3,11},{4,12},{5,13},{6,14},{7,15},{8,0},{9,1},... | collective-permute-start | bytes 393224 | tf_op jit(solution)/shard_map/ppermute | solution.py:57
  71.1 9.8 %collective-permute-start.27 = (bf16[128,512]{1,0:T(8,128)(2,1)S(1)}, bf16[128,512]{1,0:T(8,128)(2,1)S(1)}, u32[]{:S(2)}, u32[]{:S(2)}) collective-permute-start(bf16[128,512]{1,0:T(8,128)(2,1)S(1)} %get-tuple-element.29), channel_id=1, source_target_pairs={{0,12},{1,13},{2,14},{3,15},{4,0},{5,1},{6,2},{7,3},{8,4},{9,5},{1... | collective-permute-start | bytes 393224 | tf_op jit(solution)/shard_map/ppermute | solution.py:57
  (14 other events, 37.3 us)

commit v2 on v1

v2 whole, which is shorter than its diff:
```python
import math
from functools import partial

import jax
import jax.numpy as jnp
from jax import lax
from jax.experimental import pallas as pl
from jax.experimental.pallas import tpu as pltpu
from jax.sharding import PartitionSpec as P

REGRESSORS = 32
RIDGE_SCALE = 0.01
PRECISE = lax.Precision.HIGHEST
F32 = jnp.float32
BF16 = jnp.bfloat16
LANES = 128
PAD_ROWS = 16
CHUNK = 256
VMEM_BYTES = 48 * 1024 * 1024
LOG2_E = math.log2(math.e)
CONSTANT = REGRESSORS - 1


def split_bits(size):
    count = size.bit_length() - 1
    half = count // 2
    return list(range(1, half + 1)), list(range(count - 1, half, -1)) + [0]


def dot(a, b, ca=1, cb=0, precision=None):
    return lax.dot_general(
        a, b, (((ca,), (cb,)), ((), ())), precision=precision, preferred_element_type=F32
    )


def three(x, axis):
    high = x.astype(BF16)
    rest = x - high.astype(F32)
    middle = rest.astype(BF16)
    low = (rest - middle.astype(F32)).astype(BF16)
    return jnp.concatenate([high, middle, low], axis=axis)


def three_rows(x):
    blank = jnp.zeros((LANES - 3 * REGRESSORS, x.shape[1]), BF16)
    return jnp.concatenate([three(x, 0), blank], axis=0)


def lanes(shape):
    return lax.broadcasted_iota(jnp.int32, shape, len(shape) - 1)


def rows(shape):
    return lax.broadcasted_iota(jnp.int32, shape, len(shape) - 2)


def softplus(x):
    return jnp.maximum(x, 0.0) + jnp.log1p(jnp.exp(-jnp.abs(x)))


def sigmoid(x):
    small = jnp.exp(-jnp.abs(x))
    return jnp.where(x >= 0.0, 1.0, small) / (1.0 + small)


def each_chunk(size, step):
    count = size // CHUNK

    def body(i, carry):
        step(pl.ds(pl.multiple_of(i * CHUNK, CHUNK), CHUNK))
        return carry

    lax.fori_loop(0, count, body, 0, unroll=count <= 8)


def invert(matrix):
    size = matrix.shape[0]
    shape = (size, 2 * size)
    work = jnp.concatenate([matrix, jnp.eye(size, dtype=F32)], axis=1)
    row = rows(shape)
    col = lanes(shape)
    for k in range(size):
        column = jnp.sum(jnp.where(col == k, work, 0.0), axis=1, keepdims=True)
        pivot = jnp.sum(jnp.where(row == k, work, 0.0), axis=0, keepdims=True)
        pivot = pivot / jnp.sum(jnp.where(lanes(pivot.shape) == k, pivot, 0.0), axis=1, keepdims=True)
        work = jnp.where(row == k, pivot, work - column * pivot)
    return work[:, size:]


def member_kernel(set_ref, member_ref):
    label = rows((member_ref.shape[0], 1))
    member_ref[...] = jnp.where(set_ref[...] == label, 1.0, 0.0).astype(BF16)


def prepare_kernel(ridge, path_rows, small_ref, inverse_ref, design_ref, rows_ref):
    for d in range(small_ref.shape[0]):
        here = slice(d * path_rows, (d + 1) * path_rows)
        block = small_ref[d, :REGRESSORS, :path_rows]
        design_ref[:, here] = block
        turned = block.astype(F32).T
        blank = jnp.zeros((path_rows, LANES - 3 * REGRESSORS), F32)
        rows_ref[here] = jnp.concatenate([turned] * 3 + [blank], axis=1).astype(BF16)
    design = design_ref[...]
    square = (REGRESSORS, REGRESSORS)
    gram = dot(design, design, 1, 1) + jnp.where(rows(square) == lanes(square), ridge, 0.0)
    inverse_ref[...] = invert(gram)


def forward_kernel(paths, trades, *refs):
    x_refs, w_refs = refs[:paths], refs[paths : paths + trades]
    notional_ref, design_ref, member_ref, value_ref, moment_ref = refs[paths + trades :]
    weights = jnp.concatenate([w[...] for w in w_refs], axis=0)
    notional = notional_ref[...]
    start = 0
    for x in x_refs:
        pre_act = dot(x[...], weights, 1, 1)
        value_ref[start : start + x.shape[0]] = (notional * softplus(pre_act)).astype(BF16)
        start += x.shape[0]
    trade_moment = dot(design_ref[...], value_ref[...])
    parts = dot(three(trade_moment, 0), member_ref[...], 1, 1)
    moment_ref[...] = (
        parts[:REGRESSORS] + parts[REGRESSORS : 2 * REGRESSORS] + parts[2 * REGRESSORS :]
    )


def slope_kernel(paths, trades, *refs):
    x_refs, w_refs = refs[:paths], refs[paths : paths + trades]
    notional_ref, slope_ref = refs[paths + trades :]
    weights = jnp.concatenate([w[...] for w in w_refs], axis=0)
    notional = notional_ref[...]
    start = 0
    for x in x_refs:
        slope_ref[start : start + x.shape[0]] = notional * sigmoid(dot(x[...], weights, 1, 1))
        start += x.shape[0]


def solve_kernel(
    scale, paths, trades, moment_ref, inverse_ref, design_ref, rows_ref, thresh_ref, rate_ref,
    member_ref, slope_ref, *refs,
):
    x_refs = refs[:paths]
    coeffs_ref, adjoint_ref, traded_ref, slopes_ref = refs[paths : paths + 4]
    part_refs = refs[paths + 4 : paths + 4 + trades]
    turn_ref, total_ref = refs[paths + 4 + trades :]
    inverse = inverse_ref[...]
    coeffs = dot(inverse, moment_ref[...], precision=PRECISE)
    coeffs_ref[...] = coeffs
    is_constant = rows(coeffs.shape) == CONSTANT
    turn_ref[...] = three_rows(-LOG2_E * (coeffs - jnp.where(is_constant, thresh_ref[...], 0.0)))
    total_ref[...] = jnp.zeros(total_ref.shape, F32)

    def seeds(here):
        power = jnp.exp2(jnp.minimum(dot(rows_ref[here], turn_ref[...]), 126.0))
        seed = (1.0 / (1.0 + power)).astype(BF16)
        total_ref[...] += dot(design_ref[:, here], seed)

    each_chunk(rows_ref.shape[0], seeds)
    adjoint = dot(inverse, total_ref[...] * rate_ref[...], precision=PRECISE)
    adjoint_ref[...] = adjoint
    traded = dot(three_rows(adjoint), member_ref[...]).astype(BF16)
    traded_ref[...] = traded
    group = slopes_ref.shape[0]
    spread = dot(rows_ref[:group], traded).astype(BF16).astype(F32)
    slopes_ref[...] = (slope_ref[...] * spread).astype(BF16)
    basis = jnp.concatenate([x[...] for x in x_refs], axis=0)
    weight = (dot(slopes_ref[...], basis, 0, 0) * scale).astype(BF16)
    start = 0
    for part in part_refs:
        part[...] = weight[start : start + part.shape[0]]
        start += part.shape[0]


def basis_kernel(trades, slopes_ref, value_ref, traded_ref, *refs):
    w_refs, part_refs = refs[:trades], refs[trades:]
    weights = jnp.concatenate([w[...] for w in w_refs], axis=0)
    start = 0
    for part in part_refs:
        here = slice(start, start + part.shape[0])
        total = dot(slopes_ref[here], weights)
        wide = dot(value_ref[here], traded_ref[...], 1, 1)
        design = wide
        for k in range(1, 3):
            design = design + pltpu.roll(wide, LANES - k * REGRESSORS, 1)
        design = jnp.where(lanes(design.shape) < CONSTANT, design, 0.0)
        part[:, :LANES] = (total[:, :LANES] + design).astype(BF16)
        part[:, LANES:] = total[:, LANES:].astype(BF16)
        start += part.shape[0]


def loss_kernel(
    coeffs_ref, adjoint_ref, rows_ref, thresh_ref, rate_ref, loss_ref, own_ref, split_ref, total_ref
):
    coeffs = coeffs_ref[...]
    adjoint = adjoint_ref[...]
    thresh = thresh_ref[...]
    rate = rate_ref[...]
    split_ref[...] = three_rows(coeffs)
    total_ref[...] = jnp.zeros(total_ref.shape, F32)

    def losses(here):
        loss = softplus(dot(rows_ref[here], split_ref[...]) - thresh)
        total_ref[...] += jnp.sum(loss.reshape(-1, *total_ref.shape), axis=0)

    each_chunk(rows_ref.shape[0], losses)
    summed = jnp.sum(jnp.sum(total_ref[...] * rate, axis=0, keepdims=True), axis=1, keepdims=True)
    loss_ref[...] = jnp.broadcast_to(
        summed / (rows_ref.shape[0] * coeffs.shape[1]), loss_ref.shape
    )
    own = rows_ref[: own_ref.shape[0]]
    fitted = dot(own, split_ref[...])
    seed = rate * sigmoid(fitted - thresh)
    rest = seed - dot(own, three_rows(adjoint))
    design = dot(rest, coeffs, 1, 1, PRECISE) - dot(fitted, adjoint, 1, 1, PRECISE)
    blank = jnp.zeros((design.shape[0], LANES - REGRESSORS), F32)
    design = jnp.concatenate([design, blank], axis=1)
    own_ref[...] = jnp.where(lanes(design.shape) < CONSTANT, design, 0.0)


def sum_kernel(first, *refs):
    own_ref, terms = refs[0], refs[1:-2]
    basis_out_ref, weight_out_ref = refs[-2:]

    def total(parts):
        out = parts[0][...].astype(F32)
        for part in parts[1:]:
            out = out + part[...].astype(F32)
        return out

    basis = total(terms[:first])
    basis_out_ref[:, :LANES] = basis[:, :LANES] + own_ref[...]
    basis_out_ref[:, LANES:] = basis[:, LANES:]
    weight_out_ref[...] = total(terms[first:])


def call(kernel, outs, *args, name, flops=0, scratch=()):
    size = sum(a.size * a.dtype.itemsize for a in args) + sum(
        math.prod(s) * jnp.dtype(d).itemsize for s, d in outs
    )
    return pl.pallas_call(
        kernel,
        out_shape=[jax.ShapeDtypeStruct(s, d) for s, d in outs],
        in_specs=[pl.BlockSpec(memory_space=pltpu.VMEM)] * len(args),
        out_specs=[pl.BlockSpec(memory_space=pltpu.VMEM)] * len(outs),
        scratch_shapes=scratch,
        compiler_params=pltpu.CompilerParams(vmem_limit_bytes=VMEM_BYTES),
        cost_estimate=pl.CostEstimate(flops=int(flops), bytes_accessed=int(size), transcendentals=0),
        name=name,
    )(*args)


def shards(
    path_basis, proxy_weight, notional, set_of, threshold_index, threshold_levels, loss_rate
):
    n = lax.axis_size("paths")
    me = lax.axis_index("paths")
    inner_bits, outer_bits = split_bits(n)
    inner, outer = 1 << len(inner_bits), 1 << len(outer_bits)
    path_rows, features = path_basis.shape
    trade_rows = proxy_weight.shape[0]
    paths_all = path_rows * n
    sets = loss_rate.shape[0]
    group_paths, group_trades = inner * path_rows, outer * trade_rows

    def swap(x, bit):
        return lax.ppermute(x, "paths", [(d, d ^ (1 << bit)) for d in range(n)])

    def gather(x, bits):
        slots = [x]
        for bit in bits:
            slots = slots + [swap(s, bit) for s in slots]
        return slots

    def halve(slots, bits):
        slots = [[s] for s in slots]
        for bit in reversed(bits):
            count = len(slots) // 2
            for k in reversed(range(count)):
                gone = slots[count + k]
                if len(gone) > 1:
                    gone = [sum(g.astype(F32) for g in gone).astype(BF16)]
                slots[k].append(swap(gone[0], bit))
            slots = slots[:count]
        return slots[0]

    weights = gather(proxy_weight, outer_bits)
    basis = gather(path_basis, inner_bits)

    width = max(path_rows, trade_rows)
    lead = path_basis[:, :REGRESSORS].T
    lead = jnp.where(jnp.arange(REGRESSORS)[:, None] == CONSTANT, jnp.ones((), BF16), lead)
    small = jnp.concatenate(
        [
            jnp.pad(lead, ((0, 0), (0, width - path_rows))),
            jnp.pad(notional[None, :], ((0, PAD_ROWS - 1), (0, width - trade_rows))),
        ],
        axis=0,
    )[None]
    for bit in inner_bits + outer_bits:
        small = jnp.concatenate([small, swap(small, bit)], axis=0)
    design_group = jnp.concatenate([small[k, :REGRESSORS, :path_rows] for k in range(inner)], axis=1)
    notional_group = small[::inner, REGRESSORS, :trade_rows].reshape(1, group_trades).astype(F32)
    set_blocks = set_of.reshape(n, trade_rows)
    set_group = []
    for k in range(outer):
        mask = sum(((k >> j) & 1) << bit for j, bit in enumerate(outer_bits))
        set_group.append(lax.dynamic_index_in_dim(set_blocks, me ^ mask, 0))
    set_group = jnp.concatenate(set_group, axis=1)

    level = threshold_index[:, None] == jnp.arange(threshold_levels.shape[0], dtype=jnp.int32)[None, :]
    thresh = jnp.sum(jnp.where(level, threshold_levels[None, :], 0.0), axis=1)[None, :]
    rate = loss_rate[None, :]

    (member,) = call(member_kernel, [((sets, group_trades), BF16)], set_group, name="member")
    value, moment = call(
        partial(forward_kernel, inner, outer),
        [((group_paths, group_trades), BF16), ((REGRESSORS, sets), F32)],
        *basis, *weights, notional_group, design_group, member,
        name="forward",
    )
    for bit in inner_bits + outer_bits:
        moment = moment + swap(moment, bit)
    (slope,) = call(
        partial(slope_kernel, inner, outer),
        [((group_paths, group_trades), F32)],
        *basis, *weights, notional_group,
        name="slope",
    )
    inverse, design_all, design_rows = call(
        partial(prepare_kernel, RIDGE_SCALE * paths_all, path_rows),
        [((REGRESSORS, REGRESSORS), F32), ((REGRESSORS, paths_all), BF16), ((paths_all, LANES), BF16)],
        small,
        name="prepare",
    )
    coeffs, adjoint, traded, slopes, *weight_parts = call(
        partial(solve_kernel, 1.0 / math.sqrt(paths_all), inner, outer),
        [
            ((REGRESSORS, sets), F32),
            ((REGRESSORS, sets), F32),
            ((LANES, group_trades), BF16),
            ((group_paths, group_trades), BF16),
        ]
        + [((trade_rows, features), BF16)] * outer,
        moment, inverse, design_all, design_rows, thresh, rate, member, slope, *basis,
        name="solve",
        scratch=[pltpu.VMEM((LANES, sets), BF16), pltpu.VMEM((REGRESSORS, sets), F32)],
    )
    weight_terms = halve(weight_parts, outer_bits)
    basis_parts = call(
        partial(basis_kernel, outer),
        [((path_rows, features), BF16)] * inner,
        slopes, value, traded, *weights,
        name="basis_side",
    )
    basis_terms = halve(basis_parts, inner_bits)
    loss, own_adjoint = call(
        loss_kernel,
        [((8, LANES), F32), ((path_rows, LANES), F32)],
        coeffs, adjoint, design_rows, thresh, rate,
        name="loss",
        scratch=[pltpu.VMEM((LANES, sets), BF16), pltpu.VMEM((8, sets), F32)],
    )
    basis_adjoint, weight_adjoint = call(
        partial(sum_kernel, len(basis_terms)),
        [((path_rows, features), F32), ((trade_rows, features), F32)],
        own_adjoint, *basis_terms, *weight_terms,
        name="sums",
    )
    return (loss[0, :1], basis_adjoint, weight_adjoint)


def solution(mesh):
    placed = (
        P(("groups", "paths"), None),
        P(("groups", "paths"), None),
        P(("groups", "paths")),
        P("groups"),
        P("groups"),
        P("groups"),
        P("groups"),
    )
    return jax.shard_map(
        shards,
        mesh=mesh,
        in_specs=placed,
        out_specs=(P("groups"), P(("groups", "paths"), None), P(("groups", "paths"), None)),
        check_vma=False,
    )
```

time: 82.2 us -> 71.4 us (0.87)
  starting transfers between devices: 32.2 us -> 13.6 us
  waiting for transfers between devices: 19.4 us -> 37.7 us
  Pallas kernels: 0 us -> 15 us
  matrix products: 12.9 us -> 0 us
  other arithmetic: 7.76 us -> 0.34 us
  local copies, waits for them, and re-layouts: 7.6 us -> 3.58 us
  between operations: 1.82 us -> 0.86 us
    ppermute x30 -> x20, starting transfers between devices: 32.2 us -> 13.6 us  [swap(): return lax.ppermute(x, 'paths', [(d, d ^ 1 << bit) for d in range(n)])]
    ppermute x30 -> x20, waiting for transfers between devices: 19.4 us -> 37.7 us  [swap(): return lax.ppermute(x, 'paths', [(d, d ^ 1 << bit) for d in range(n)])]
    pallas_call x0 -> x8, Pallas kernels: none -> 15 us  [call(): pl.pallas_call(kernel, out_shape=[jax.ShapeDtypeStruct(s, d) for s, d in...]
    dot_general x14 -> x0, matrix products: 12.2 us -> none  [dot_dims(): lax.dot_general(a, b, (((ca,), (cb,)), ((), ())), precision=precision, pr...]
    another operation x7 -> x0, other arithmetic: 6.69 us -> none  [the longest x3 3.59 us: spd_solve(): lower_factor = jnp.linalg.cholesky(matrix)]
    unnamed x22 -> x16, local copies, waits for them, and re-layouts: 3.07 us -> 1.48 us
    slice x6 -> x2, local copies, waits for them, and re-layouts: 2.02 us -> 1.3 us  [the longest x1 0.79 us: shards(): lead = path_basis[:, :REGRESSORS].T]
  transfers between devices with their start and end apart: 30 -> 20, of which waited for: 12 -> 12; matrix products, arithmetic and copies ran while one was open for 14% -> 3% of each run, Pallas kernels for 0% -> 12%
where the time goes in v2:
time: 71.4 us; the launch traced here: 71.2 us
  waiting for transfers between devices  37.7 us (53%)
  Pallas kernels  15 us (21%)
  starting transfers between devices  13.6 us (19%)
  local copies, waits for them, and re-layouts  3.58 us (5%)
  between operations  0.86 us (1%)
    ppermute x20, waiting for transfers between devices, swap(): return lax.ppermute(x, 'paths', [(d, d ^ 1 << bit) for d in range(n)])  37.7 us
    pallas_call x8, Pallas kernels, call(): pl.pallas_call(kernel, out_shape=[jax.ShapeDtypeStruct(s, d) for s, d in...  15 us
    ppermute x20, starting transfers between devices, swap(): return lax.ppermute(x, 'paths', [(d, d ^ 1 << bit) for d in range(n)])  13.6 us
    unnamed x16, local copies, waits for them, and re-layouts  1.48 us
  transfers between devices with their start and end apart: 20, of which 12 were waited for; matrix products, arithmetic and copies ran while one was open for 3% of the time, Pallas kernels for 12%

profile of v2, /device:TPU:0, one launch (start us, length us, event | category | flops | bytes accessed | tf_op | source)
XLA Modules:
  0.0 71.2 jit_solution(18075387762549327921)
XLA Ops:
  1.1 3.7 %collective-permute-start.3 = (bf16[128,512]{1,0:T(8,128)(2,1)}, bf16[128,512]{1,0:T(8,128)(2,1)S(1)}, u32[]{:S(2)}, u32[]{:S(2)}) collective-permute-start(bf16[128,512]{1,0:T(8,128)(2,1)} %refs_0_.7), channel_id=1, source_target_pairs={{0,8},{1,9},{2,10},{3,11},{4,12},{5,13},{6,14},{7,15},{8,0},{9,1},... | collective-permute-start | bytes 393224 | tf_op jit(solution)/shard_map/ppermute | solution.py:265
  4.8 1.6 %collective-permute-start.1 = (bf16[128,512]{1,0:T(8,128)(2,1)}, bf16[128,512]{1,0:T(8,128)(2,1)S(1)}, u32[]{:S(2)}, u32[]{:S(2)}) collective-permute-start(bf16[128,512]{1,0:T(8,128)(2,1)} %refs_0_.6), channel_id=1, source_target_pairs={{0,4},{1,5},{2,6},{3,7},{4,0},{5,1},{6,2},{7,3},{8,12},{9,13},{10,... | collective-permute-start | bytes 393224 | tf_op jit(solution)/shard_map/ppermute | solution.py:265
  6.4 1.5 %collective-permute-start = (bf16[128,512]{1,0:T(8,128)(2,1)}, bf16[128,512]{1,0:T(8,128)(2,1)S(1)}, u32[]{:S(2)}, u32[]{:S(2)}) collective-permute-start(bf16[128,512]{1,0:T(8,128)(2,1)} %refs_0_.6), channel_id=1, source_target_pairs={{0,2},{1,3},{2,0},{3,1},{4,6},{5,7},{6,4},{7,5},{8,10},{9,11},{10,... | collective-permute-start | bytes 393224 | tf_op jit(solution)/shard_map/ppermute | solution.py:265
  7.9 0.8 %slice.21 = bf16[128,32]{1,0:T(8,128)(2,1)S(1)} slice(bf16[128,512]{1,0:T(8,128)(2,1)} %refs_0_.6), slice={[0:128], [0:32]} | slice | bytes 16384 | tf_op jit(solution)/shard_map/slice | solution.py:289
  8.9 0.7 copy-done.4
  10.1 0.8 %constant_dynamic-slice_fusion.3 = (s32[1,128]{1,0:T(1,128)S(1)}, s32[1,128]{1,0:T(1,128)S(1)}, s32[1,128]{1,0:T(1,128)S(1)}, s32[1,128]{1,0:T(1,128)S(1)}) fusion(s32[16,128]{1,0:T(8,128)} %bitcast.28, s32[]{:T(128)S(6)} %select_n.26, s32[]{:T(128)S(6)} %select_n.29, s32[]{:T(128)S(6)} %select_n.28, s32[]{:T(128)S(6)} %select_n.27), kind=kLoop, calls=%fused_computation.27 | loop fusion | bytes 4112 | tf_op jit(solution)/shard_map/jit(dynamic_index_in_dim)/dynamic_slice | solution.py:306
  10.9 2.3 %collective-permute-done.6 = bf16[1,48,128]{2,1,0:T(8,128)(2,1)S(1)} collective-permute-done((bf16[1,48,128]{2,1,0:T(8,128)(2,1)S(1)}, bf16[1,48,128]{2,1,0:T(8,128)(2,1)S(1)}, u32[]{:S(2)}, u32[]{:S(2)}) %collective-permute-start.6) | collective-permute-done | bytes 12320 | tf_op jit(solution)/shard_map/ppermute | solution.py:265
  13.7 3.4 %collective-permute-done.7 = bf16[2,48,128]{2,1,0:T(8,128)(2,1)S(1)} collective-permute-done((bf16[2,48,128]{2,1,0:T(8,128)(2,1)S(1)}, bf16[2,48,128]{2,1,0:T(8,128)(2,1)S(1)}, u32[]{:S(2)}, u32[]{:S(2)}) %collective-permute-start.7) | collective-permute-done | bytes 24608 | tf_op jit(solution)/shard_map/ppermute | solution.py:265
  17.5 5.0 %collective-permute-done.8 = bf16[4,48,128]{2,1,0:T(8,128)(2,1)S(1)} collective-permute-done((bf16[4,48,128]{2,1,0:T(8,128)(2,1)S(1)}, bf16[4,48,128]{2,1,0:T(8,128)(2,1)S(1)}, u32[]{:S(2)}, u32[]{:S(2)}) %collective-permute-start.8) | collective-permute-done | bytes 49184 | tf_op jit(solution)/shard_map/ppermute | solution.py:265
  24.2 4.5 %collective-permute-done.2.refs_3_ = bf16[128,512]{1,0:T(8,128)(2,1)S(1)} collective-permute-done((bf16[128,512]{1,0:T(8,128)(2,1)S(1)}, bf16[128,512]{1,0:T(8,128)(2,1)S(1)}, u32[]{:S(2)}, u32[]{:S(2)}) %collective-permute-start.2) | collective-permute-done | bytes 131104 | tf_op jit(solution)/shard_map/ppermute | solution.py:265
  28.7 1.3 %forward.1 = (bf16[512,512]{1,0:T(8,128)(2,1)S(1)}, f32[32,512]{1,0:T(8,128)S(1)}) custom-call(bf16[128,512]{1,0:T(8,128)(2,1)S(1)} %copy-done, bf16[128,512]{1,0:T(8,128)(2,1)S(1)} %collective-permute-done.refs_1_, bf16[128,512]{1,0:T(8,128)(2,1)S(1)} %collective-permute-done.1.refs_2_, bf16[128,512]{1,0:T(8,128)(2,1)S(1)} %collective-permute-done.2.refs_3_, ...), custom_call_target="tpu_custom_call" | custom-call | bytes 2197504 | tf_op jit(solution)/shard_map/forward/pallas_call | solution.py:239
  30.6 3.8 %collective-permute-done.10 = f32[32,512]{1,0:T(8,128)S(1)} collective-permute-done((f32[32,512]{1,0:T(8,128)S(1)}, f32[32,512]{1,0:T(8,128)S(1)}, u32[]{:S(2)}, u32[]{:S(2)}) %collective-permute-start.10) | collective-permute-done | bytes 65568 | tf_op jit(solution)/shard_map/ppermute | solution.py:265
  34.7 4.0 %collective-permute-done.11 = f32[32,512]{1,0:T(8,128)S(1)} collective-permute-done((f32[32,512]{1,0:T(8,128)S(1)}, f32[32,512]{1,0:T(8,128)S(1)}, u32[]{:S(2)}, u32[]{:S(2)}) %collective-permute-start.11) | collective-permute-done | bytes 65568 | tf_op jit(solution)/shard_map/ppermute | solution.py:265
  38.8 5.9 %collective-permute-done.12 = f32[32,512]{1,0:T(8,128)S(1)} collective-permute-done((f32[32,512]{1,0:T(8,128)S(1)}, f32[32,512]{1,0:T(8,128)S(1)}, u32[]{:S(2)}, u32[]{:S(2)}) %collective-permute-start.12) | collective-permute-done | bytes 65568 | tf_op jit(solution)/shard_map/ppermute | solution.py:265
  44.8 4.4 %prepare.1 = (f32[32,32]{1,0:T(8,128)S(1)}, bf16[32,2048]{1,0:T(8,128)(2,1)S(1)}, bf16[2048,128]{1,0:T(8,128)(2,1)S(1)}) custom-call(bf16[16,48,128]{2,1,0:T(8,128)(2,1)S(1)} %constant_dynamic-update-slice_fusion.small_ref), custom_call_target="tpu_custom_call" | custom-call | bytes 856064 | tf_op jit(solution)/shard_map/prepare/pallas_call | solution.py:239
  49.3 0.9 %slope.1.slope_ref = f32[512,512]{1,0:T(8,128)S(1)} custom-call(bf16[128,512]{1,0:T(8,128)(2,1)S(1)} %copy-done, bf16[128,512]{1,0:T(8,128)(2,1)S(1)} %collective-permute-done.refs_1_, bf16[128,512]{1,0:T(8,128)(2,1)S(1)} %collective-permute-done.1.refs_2_, bf16[128,512]{1,0:T(8,128)(2,1)S(1)} %collective-permute-done.2.refs_3_, ...), custom_call_target="tpu_custom_call" | custom-call | bytes 2099200 | tf_op jit(solution)/shard_map/slope/pallas_call | solution.py:239
  50.2 0.7 copy-done.2
  50.9 3.7 %solve.1 = (f32[32,512]{1,0:T(8,128)S(1)}, f32[32,512]{1,0:T(8,128)S(1)}, bf16[128,512]{1,0:T(8,128)(2,1)S(1)}, bf16[512,512]{1,0:T(8,128)(2,1)S(1)}, bf16[128,5...) custom-call(f32[32,512]{1,0:T(8,128)S(1)} %add.40.moment_ref, ...), custom_call_target="tpu_custom_call" | custom-call | bytes 4136960 | tf_op jit(solution)/shard_map/solve/pallas_call | solution.py:239
  54.6 0.7 basis_side.1
  55.4 1.9 %collective-permute-start.14 = (bf16[128,512]{1,0:T(8,128)(2,1)S(1)}, bf16[128,512]{1,0:T(8,128)(2,1)S(1)}, u32[]{:S(2)}, u32[]{:S(2)}) collective-permute-start(bf16[128,512]{1,0:T(8,128)(2,1)S(1)} %get-tuple-element.36), channel_id=1, source_target_pairs={{0,4},{1,5},{2,6},{3,7},{4,0},{5,1},{6,2},{7,3},{8,12},{9,13},{10,... | collective-permute-start | bytes 393224 | tf_op jit(solution)/shard_map/ppermute | solution.py:265
  57.8 3.8 %collective-permute-done.15 = bf16[128,512]{1,0:T(8,128)(2,1)S(1)} collective-permute-done((bf16[128,512]{1,0:T(8,128)(2,1)S(1)}, bf16[128,512]{1,0:T(8,128)(2,1)S(1)}, u32[]{:S(2)}, u32[]{:S(2)}) %collective-permute-start.15) | collective-permute-done | bytes 131104 | tf_op jit(solution)/shard_map/ppermute | solution.py:265
  62.3 3.2 %loss.1 = (f32[8,128]{1,0:T(8,128)S(1)}, f32[128,128]{1,0:T(8,128)S(1)}) custom-call(f32[32,512]{1,0:T(8,128)S(1)} %get-tuple-element.28.coeffs_ref, f32[32,512]{1,0:T(8,128)S(1)} %get-tuple-element.29.adjoint_ref, bf16[2048,128]{1,0:T(8,128)(2,1)S(1)} %get-tuple-element.27.rows_ref, f32[1,512]{1,0:T(1,128)S(1)} %bitcast.23, f32[1,512]{1,0:T(1,128)S(1)} %bitcast.25), custom_call_target="tpu_custom_call" | custom-call | bytes 729088 | tf_op jit(solution)/shard_map/loss/pallas_call | solution.py:239
  66.7 3.7 %collective-permute-done.19.refs_6_ = bf16[128,512]{1,0:T(8,128)(2,1)S(1)} collective-permute-done((bf16[128,512]{1,0:T(8,128)(2,1)S(1)}, bf16[128,512]{1,0:T(8,128)(2,1)S(1)}, u32[]{:S(2)}, u32[]{:S(2)}) %collective-permute-start.19) | collective-permute-done | bytes 131104 | tf_op jit(solution)/shard_map/ppermute | solution.py:265
  70.3 0.8 %sums.1 = (f32[128,512]{1,0:T(8,128)}, f32[128,512]{1,0:T(8,128)}) custom-call(f32[128,128]{1,0:T(8,128)S(1)} %get-tuple-element.31.refs_0_, bf16[128,512]{1,0:T(8,128)(2,1)S(1)} %get-tuple-element.35.refs_1_, bf16[128,512]{1,0:T(8,128)(2,1)S(1)} %collective-permute-done.14.refs_2_, bf16[128,512]{1,0:T(8,128)(2,1)S(1)} %collective-permute-done.16.refs_3_, ...), custom_call_target="tpu_custom_call" | custom-call | bytes 1376256 | tf_op jit(solution)/shard_map/sums/pallas_call | solution.py:239
  (64 shorter events, 7.6 us)
Async XLA Ops:
  0.6 23.4 %collective-permute-start.4 = (bf16[128,512]{1,0:T(8,128)(2,1)}, bf16[128,512]{1,0:T(8,128)(2,1)S(1)}, u32[]{:S(2)}, u32[]{:S(2)}) collective-permute-start(bf16[128,512]{1,0:T(8,128)(2,1)} %refs_0_.7), channel_id=1, source_target_pairs={{0,1},{1,0},{2,3},{3,2},{4,5},{5,4},{6,7},{7,6},{8,9},{9,8},{10,11... | collective-permute-start | bytes 393224 | tf_op jit(solution)/shard_map/ppermute | solution.py:265
  1.1 21.5 %collective-permute-start.3 = (bf16[128,512]{1,0:T(8,128)(2,1)}, bf16[128,512]{1,0:T(8,128)(2,1)S(1)}, u32[]{:S(2)}, u32[]{:S(2)}) collective-permute-start(bf16[128,512]{1,0:T(8,128)(2,1)} %refs_0_.7), channel_id=1, source_target_pairs={{0,8},{1,9},{2,10},{3,11},{4,12},{5,13},{6,14},{7,15},{8,0},{9,1},... | collective-permute-start | bytes 393224 | tf_op jit(solution)/shard_map/ppermute | solution.py:265
  4.8 19.2 %collective-permute-start.1 = (bf16[128,512]{1,0:T(8,128)(2,1)}, bf16[128,512]{1,0:T(8,128)(2,1)S(1)}, u32[]{:S(2)}, u32[]{:S(2)}) collective-permute-start(bf16[128,512]{1,0:T(8,128)(2,1)} %refs_0_.6), channel_id=1, source_target_pairs={{0,4},{1,5},{2,6},{3,7},{4,0},{5,1},{6,2},{7,3},{8,12},{9,13},{10,... | collective-permute-start | bytes 393224 | tf_op jit(solution)/shard_map/ppermute | solution.py:265
  6.4 16.9 %collective-permute-start = (bf16[128,512]{1,0:T(8,128)(2,1)}, bf16[128,512]{1,0:T(8,128)(2,1)S(1)}, u32[]{:S(2)}, u32[]{:S(2)}) collective-permute-start(bf16[128,512]{1,0:T(8,128)(2,1)} %refs_0_.6), channel_id=1, source_target_pairs={{0,2},{1,3},{2,0},{3,1},{4,6},{5,7},{6,4},{7,5},{8,10},{9,11},{10,... | collective-permute-start | bytes 393224 | tf_op jit(solution)/shard_map/ppermute | solution.py:265
  9.5 3.7 %collective-permute-start.6 = (bf16[1,48,128]{2,1,0:T(8,128)(2,1)S(1)}, bf16[1,48,128]{2,1,0:T(8,128)(2,1)S(1)}, u32[]{:S(2)}, u32[]{:S(2)}) collective-permute-start(bf16[1,48,128]{2,1,0:T(8,128)(2,1)S(1)} %fusion.2), channel_id=1, source_target_pairs={{0,2},{1,3},{2,0},{3,1},{4,6},{5,7},{6,4},{7,5},{8,10},{9,11},{10,... | collective-permute-start | bytes 36872 | tf_op jit(solution)/shard_map/ppermute | solution.py:265
  13.2 3.8 %collective-permute-start.7 = (bf16[2,48,128]{2,1,0:T(8,128)(2,1)S(1)}, bf16[2,48,128]{2,1,0:T(8,128)(2,1)S(1)}, u32[]{:S(2)}, u32[]{:S(2)}) collective-permute-start(bf16[2,48,128]{2,1,0:T(8,128)(2,1)S(1)} %pad_maximum_fusion.3), channel_id=1, source_target_pairs={{0,4},{1,5},{2,6},{3,7},{4,0},{5,1},{6,2},{7,3},{8,12},{9,13},{10,... | collective-permute-start | bytes 73736 | tf_op jit(solution)/shard_map/ppermute | solution.py:265
  17.1 5.5 %collective-permute-start.8 = (bf16[4,48,128]{2,1,0:T(8,128)(2,1)S(1)}, bf16[4,48,128]{2,1,0:T(8,128)(2,1)S(1)}, u32[]{:S(2)}, u32[]{:S(2)}) collective-permute-start(bf16[4,48,128]{2,1,0:T(8,128)(2,1)S(1)} %pad_maximum_fusion.1), channel_id=1, source_target_pairs={{0,8},{1,9},{2,10},{3,11},{4,12},{5,13},{6,14},{7,15},{8,0},{9,1},... | collective-permute-start | bytes 147464 | tf_op jit(solution)/shard_map/ppermute | solution.py:265
  22.6 6.2 %copy-start = (bf16[128,512]{1,0:T(8,128)(2,1)S(1)}, bf16[128,512]{1,0:T(8,128)(2,1)}, u32[]{:S(2)}) copy-start(bf16[128,512]{1,0:T(8,128)(2,1)} %refs_0_.6) | copy-start | bytes 393220
  22.6 6.2 %copy-start.1 = (bf16[128,512]{1,0:T(8,128)(2,1)S(1)}, bf16[128,512]{1,0:T(8,128)(2,1)}, u32[]{:S(2)}) copy-start(bf16[128,512]{1,0:T(8,128)(2,1)} %refs_0_.7) | copy-start | bytes 393220
  22.6 1.4 %collective-permute-start.9 = (bf16[8,48,128]{2,1,0:T(8,128)(2,1)S(1)}, bf16[8,48,128]{2,1,0:T(8,128)(2,1)S(1)}, u32[]{:S(2)}, u32[]{:S(2)}) collective-permute-start(bf16[8,48,128]{2,1,0:T(8,128)(2,1)S(1)} %pad_maximum_fusion), channel_id=1, source_target_pairs={{0,1},{1,0},{2,3},{3,2},{4,5},{5,4},{6,7},{7,6},{8,9},{9,8},{10,11... | collective-permute-start | bytes 294920 | tf_op jit(solution)/shard_map/ppermute | solution.py:265
  22.7 1.5 %collective-permute-start.5 = (bf16[128,512]{1,0:T(8,128)(2,1)S(1)}, bf16[128,512]{1,0:T(8,128)(2,1)S(1)}, u32[]{:S(2)}, u32[]{:S(2)}) collective-permute-start(bf16[128,512]{1,0:T(8,128)(2,1)S(1)} %collective-permute-done.3.refs_5_.refs_1_), channel_id=1, source_target_pairs={{0,1},{1,0},{2,3},{3,2},{4,5},{5,4},{6,7},{7,6},{8,9},{9,8},{10,11... | collective-permute-start | bytes 393224 | tf_op jit(solution)/shard_map/ppermute | solution.py:265
  23.3 5.5 %collective-permute-start.2 = (bf16[128,512]{1,0:T(8,128)(2,1)S(1)}, bf16[128,512]{1,0:T(8,128)(2,1)S(1)}, u32[]{:S(2)}, u32[]{:S(2)}) collective-permute-start(bf16[128,512]{1,0:T(8,128)(2,1)S(1)} %collective-permute-done.refs_1_), channel_id=1, source_target_pairs={{0,4},{1,5},{2,6},{3,7},{4,0},{5,1},{6,2},{7,3},{8,12},{9,13},{10,... | collective-permute-start | bytes 393224 | tf_op jit(solution)/shard_map/ppermute | solution.py:265
  30.0 4.3 %collective-permute-start.10 = (f32[32,512]{1,0:T(8,128)S(1)}, f32[32,512]{1,0:T(8,128)S(1)}, u32[]{:S(2)}, u32[]{:S(2)}) collective-permute-start(f32[32,512]{1,0:T(8,128)S(1)} %get-tuple-element.24), channel_id=1, source_target_pairs={{0,2},{1,3},{2,0},{3,1},{4,6},{5,7},{6,4},{7,5},{8,10},{9,11},{10,... | collective-permute-start | bytes 196616 | tf_op jit(solution)/shard_map/ppermute | solution.py:265
  34.3 4.3 %collective-permute-start.11 = (f32[32,512]{1,0:T(8,128)S(1)}, f32[32,512]{1,0:T(8,128)S(1)}, u32[]{:S(2)}, u32[]{:S(2)}) collective-permute-start(f32[32,512]{1,0:T(8,128)S(1)} %add.37), channel_id=1, source_target_pairs={{0,4},{1,5},{2,6},{3,7},{4,0},{5,1},{6,2},{7,3},{8,12},{9,13},{10,... | collective-permute-start | bytes 196616 | tf_op jit(solution)/shard_map/ppermute | solution.py:265
  38.7 6.1 %copy-start.3 = (s32[512]{0:T(512)S(1)}, s32[512]{0:T(512)}, u32[]{:S(2)}) copy-start(s32[512]{0:T(512)} %param.11) | copy-start | bytes 6148
  38.7 6.0 %copy-start.5 = (f32[16]{0:T(128)S(1)}, f32[16]{0:T(128)}, u32[]{:S(2)}) copy-start(f32[16]{0:T(128)} %param.12) | copy-start | bytes 196
  38.7 5.9 %collective-permute-start.12 = (f32[32,512]{1,0:T(8,128)S(1)}, f32[32,512]{1,0:T(8,128)S(1)}, u32[]{:S(2)}, u32[]{:S(2)}) collective-permute-start(f32[32,512]{1,0:T(8,128)S(1)} %add.38), channel_id=1, source_target_pairs={{0,8},{1,9},{2,10},{3,11},{4,12},{5,13},{6,14},{7,15},{8,0},{9,1},... | collective-permute-start | bytes 196616 | tf_op jit(solution)/shard_map/ppermute | solution.py:265
  44.7 5.5 %collective-permute-start.13 = (f32[32,512]{1,0:T(8,128)S(1)}, f32[32,512]{1,0:T(8,128)S(1)}, u32[]{:S(2)}, u32[]{:S(2)}) collective-permute-start(f32[32,512]{1,0:T(8,128)S(1)} %add.39), channel_id=1, source_target_pairs={{0,1},{1,0},{2,3},{3,2},{4,5},{5,4},{6,7},{7,6},{8,9},{9,8},{10,11... | collective-permute-start | bytes 196616 | tf_op jit(solution)/shard_map/ppermute | solution.py:265
  55.2 6.4 %collective-permute-start.15 = (bf16[128,512]{1,0:T(8,128)(2,1)S(1)}, bf16[128,512]{1,0:T(8,128)(2,1)S(1)}, u32[]{:S(2)}, u32[]{:S(2)}) collective-permute-start(bf16[128,512]{1,0:T(8,128)(2,1)S(1)} %get-tuple-element.38), channel_id=1, source_target_pairs={{0,4},{1,5},{2,6},{3,7},{4,0},{5,1},{6,2},{7,3},{8,12},{9,13},{10,... | collective-permute-start | bytes 393224 | tf_op jit(solution)/shard_map/ppermute | solution.py:265
  55.4 10.6 %collective-permute-start.14 = (bf16[128,512]{1,0:T(8,128)(2,1)S(1)}, bf16[128,512]{1,0:T(8,128)(2,1)S(1)}, u32[]{:S(2)}, u32[]{:S(2)}) collective-permute-start(bf16[128,512]{1,0:T(8,128)(2,1)S(1)} %get-tuple-element.36), channel_id=1, source_target_pairs={{0,4},{1,5},{2,6},{3,7},{4,0},{5,1},{6,2},{7,3},{8,12},{9,13},{10,... | collective-permute-start | bytes 393224 | tf_op jit(solution)/shard_map/ppermute | solution.py:265
  57.3 8.7 %collective-permute-start.17 = (bf16[128,512]{1,0:T(8,128)(2,1)S(1)}, bf16[128,512]{1,0:T(8,128)(2,1)S(1)}, u32[]{:S(2)}, u32[]{:S(2)}) collective-permute-start(bf16[128,512]{1,0:T(8,128)(2,1)S(1)} %get-tuple-element.40), channel_id=1, source_target_pairs={{0,1},{1,0},{2,3},{3,2},{4,5},{5,4},{6,7},{7,6},{8,9},{9,8},{10,11... | collective-permute-start | bytes 393224 | tf_op jit(solution)/shard_map/ppermute | solution.py:265
  57.3 4.9 %collective-permute-start.18 = (bf16[128,512]{1,0:T(8,128)(2,1)S(1)}, bf16[128,512]{1,0:T(8,128)(2,1)S(1)}, u32[]{:S(2)}, u32[]{:S(2)}) collective-permute-start(bf16[128,512]{1,0:T(8,128)(2,1)S(1)} %get-tuple-element.42), channel_id=1, source_target_pairs={{0,1},{1,0},{2,3},{3,2},{4,5},{5,4},{6,7},{7,6},{8,9},{9,8},{10,11... | collective-permute-start | bytes 393224 | tf_op jit(solution)/shard_map/ppermute | solution.py:265
  61.6 5.0 %collective-permute-start.16 = (bf16[128,512]{1,0:T(8,128)(2,1)S(1)}, bf16[128,512]{1,0:T(8,128)(2,1)S(1)}, u32[]{:S(2)}, u32[]{:S(2)}) collective-permute-start(bf16[128,512]{1,0:T(8,128)(2,1)S(1)} %add_convert_fusion.1), channel_id=1, source_target_pairs={{0,2},{1,3},{2,0},{3,1},{4,6},{5,7},{6,4},{7,5},{8,10},{9,11},{10,... | collective-permute-start | bytes 393224 | tf_op jit(solution)/shard_map/ppermute | solution.py:265
  62.2 8.1 %collective-permute-start.19 = (bf16[128,512]{1,0:T(8,128)(2,1)S(1)}, bf16[128,512]{1,0:T(8,128)(2,1)S(1)}, u32[]{:S(2)}, u32[]{:S(2)}) collective-permute-start(bf16[128,512]{1,0:T(8,128)(2,1)S(1)} %add_convert_fusion), channel_id=1, source_target_pairs={{0,8},{1,9},{2,10},{3,11},{4,12},{5,13},{6,14},{7,15},{8,0},{9,1},... | collective-permute-start | bytes 393224 | tf_op jit(solution)/shard_map/ppermute | solution.py:265
  (2 other events, 1.4 us)

commit v3 on v2

v3 whole, which is shorter than its diff:
```python
import math
from functools import partial

import jax
import jax.numpy as jnp
from jax import lax
from jax.experimental import pallas as pl
from jax.experimental.pallas import tpu as pltpu
from jax.sharding import PartitionSpec as P

REGRESSORS = 32
RIDGE_SCALE = 0.01
PRECISE = lax.Precision.HIGHEST
F32 = jnp.float32
BF16 = jnp.bfloat16
LANES = 128
PAD_ROWS = 16
CHUNK = 256
VMEM_BYTES = 48 * 1024 * 1024
LOG2_E = math.log2(math.e)
CONSTANT = REGRESSORS - 1


def split_bits(size):
    count = size.bit_length() - 1
    half = count // 2
    return list(range(1, half + 1)), list(range(count - 1, half, -1)) + [0]


def dot(a, b, ca=1, cb=0, precision=None):
    return lax.dot_general(
        a, b, (((ca,), (cb,)), ((), ())), precision=precision, preferred_element_type=F32
    )


def three(x, axis):
    high = x.astype(BF16)
    rest = x - high.astype(F32)
    middle = rest.astype(BF16)
    low = (rest - middle.astype(F32)).astype(BF16)
    return jnp.concatenate([high, middle, low], axis=axis)


def three_rows(x):
    blank = jnp.zeros((LANES - 3 * REGRESSORS, x.shape[1]), BF16)
    return jnp.concatenate([three(x, 0), blank], axis=0)


def lanes(shape):
    return lax.broadcasted_iota(jnp.int32, shape, len(shape) - 1)


def rows(shape):
    return lax.broadcasted_iota(jnp.int32, shape, len(shape) - 2)


def softplus(x):
    return jnp.maximum(x, 0.0) + jnp.log1p(jnp.exp(-jnp.abs(x)))


def sigmoid(x):
    small = jnp.exp(-jnp.abs(x))
    return jnp.where(x >= 0.0, 1.0, small) / (1.0 + small)


def each_chunk(size, step):
    count = size // CHUNK

    def body(i, carry):
        step(pl.ds(pl.multiple_of(i * CHUNK, CHUNK), CHUNK))
        return carry

    lax.fori_loop(0, count, body, 0, unroll=count <= 8)


def invert(matrix):
    size = matrix.shape[0]
    work = jnp.concatenate([matrix, jnp.eye(size, dtype=F32)], axis=1)
    row = rows((size, 2 * size))
    for k in range(size):
        pivot = work[k : k + 1] / work[k : k + 1, k : k + 1]
        work = jnp.where(row == k, pivot, work - work[:, k : k + 1] * pivot)
    return work[:, size:]


def tables_kernel(
    trade_masks, inner, me_ref, level_ref, set_ref, index_ref, rate_ref,
    member_ref, thresh_out_ref, rate_out_ref,
):
    me = me_ref[0]
    place = (me >> 1) & (inner - 1)
    size = member_ref.shape[0] // inner
    trades = set_ref.shape[-1]
    for m in range(inner):
        here = slice(m * size, (m + 1) * size)
        label = (place ^ m) * size + rows((size, 1))
        for j, mask in enumerate(trade_masks):
            member_ref[here, j * trades : (j + 1) * trades] = jnp.where(
                set_ref[me ^ mask] == label, 1.0, 0.0
            ).astype(BF16)
        index = index_ref[place ^ m]
        thresh = jnp.zeros(index.shape, F32)
        for k in range(level_ref.shape[0]):
            thresh = jnp.where(index == k, level_ref[k], thresh)
        thresh_out_ref[:, here] = thresh
        rate_out_ref[:, here] = rate_ref[place ^ m]


def design_kernel(path_rows, small_ref, design_ref, rows_ref):
    for d in range(small_ref.shape[0]):
        here = slice(d * path_rows, (d + 1) * path_rows)
        block = small_ref[d, :REGRESSORS, :path_rows]
        design_ref[:, here] = block
        turned = block.astype(F32).T
        blank = jnp.zeros((path_rows, LANES - 3 * REGRESSORS), F32)
        rows_ref[here] = jnp.concatenate([turned] * 3 + [blank], axis=1).astype(BF16)


def inverse_kernel(ridge, path_rows, small_ref, inverse_ref):
    square = (REGRESSORS, REGRESSORS)
    gram = jnp.where(rows(square) == lanes(square), ridge, 0.0)
    for d in range(small_ref.shape[0]):
        block = small_ref[d, :REGRESSORS, :path_rows]
        gram = gram + dot(block, block, 1, 1)
    inverse_ref[...] = invert(gram)


def forward_kernel(paths, trades, *refs):
    x_refs, w_refs = refs[:paths], refs[paths : paths + trades]
    notional_ref, design_ref, member_ref, value_ref, *moment_refs = refs[paths + trades :]
    weights = jnp.concatenate([w[...] for w in w_refs], axis=0)
    notional = notional_ref[...]
    start = 0
    for x in x_refs:
        pre_act = dot(x[...], weights, 1, 1)
        value_ref[start : start + x.shape[0]] = (notional * softplus(pre_act)).astype(BF16)
        start += x.shape[0]
    trade_moment = dot(design_ref[...], value_ref[...])
    parts = dot(three(trade_moment, 0), member_ref[...], 1, 1)
    moment = parts[:REGRESSORS] + parts[REGRESSORS : 2 * REGRESSORS] + parts[2 * REGRESSORS :]
    size = moment.shape[1] // len(moment_refs)
    for m, moment_ref in enumerate(moment_refs):
        moment_ref[...] = moment[:, m * size : (m + 1) * size]


def slope_kernel(paths, trades, *refs):
    x_refs, w_refs = refs[:paths], refs[paths : paths + trades]
    notional_ref, slope_ref = refs[paths + trades :]
    weights = jnp.concatenate([w[...] for w in w_refs], axis=0)
    notional = notional_ref[...]
    start = 0
    for x in x_refs:
        slope_ref[start : start + x.shape[0]] = notional * sigmoid(dot(x[...], weights, 1, 1))
        start += x.shape[0]


def solve_kernel(
    terms, inverse_ref, design_ref, rows_ref, thresh_ref, rate_ref, *refs
):
    solved_ref, turn_ref, total_ref = refs[terms:]
    moment = refs[0][...]
    for ref in refs[1:terms]:
        moment = moment + ref[...]
    size = moment.shape[1]
    inverse = inverse_ref[...]
    coeffs = dot(inverse, moment, precision=PRECISE)
    solved_ref[REGRESSORS:] = coeffs
    is_constant = rows(coeffs.shape) == CONSTANT
    shifted = coeffs - jnp.where(is_constant, thresh_ref[:, :size], 0.0)
    turn_ref[...] = three_rows(-LOG2_E * shifted)
    total_ref[...] = jnp.zeros(total_ref.shape, F32)

    def seeds(here):
        power = jnp.exp2(jnp.minimum(dot(rows_ref[here], turn_ref[...]), 126.0))
        seed = (1.0 / (1.0 + power)).astype(BF16)
        total_ref[...] += dot(design_ref[:, here], seed)

    each_chunk(rows_ref.shape[0], seeds)
    solved_ref[:REGRESSORS] = dot(inverse, total_ref[...] * rate_ref[:, :size], precision=PRECISE)


def joined(refs, part):
    here = slice(part * REGRESSORS, (part + 1) * REGRESSORS)
    return jnp.concatenate([ref[here] for ref in refs], axis=1)


def backward_kernel(scale, paths, trades, member_ref, rows_ref, slope_ref, value_ref, *refs):
    solved_refs, refs = refs[:paths], refs[paths:]
    x_refs, refs = refs[:paths], refs[paths:]
    w_refs, refs = refs[:trades], refs[trades:]
    weight_refs, basis_refs, slopes_ref = refs[:trades], refs[trades:-1], refs[-1]
    traded = dot(three_rows(joined(solved_refs, 0)), member_ref[...]).astype(BF16)
    group = slopes_ref.shape[0]
    spread = dot(rows_ref[:group], traded).astype(BF16).astype(F32)
    slopes_ref[...] = (slope_ref[...] * spread).astype(BF16)
    basis = jnp.concatenate([x[...] for x in x_refs], axis=0)
    weight = (dot(slopes_ref[...], basis, 0, 0) * scale).astype(BF16)
    start = 0
    for part in weight_refs:
        part[...] = weight[start : start + part.shape[0]]
        start += part.shape[0]
    weights = jnp.concatenate([w[...] for w in w_refs], axis=0)
    start = 0
    for part in basis_refs:
        here = slice(start, start + part.shape[0])
        total = dot(slopes_ref[here], weights)
        wide = dot(value_ref[here], traded, 1, 1)
        design = wide
        for k in range(1, 3):
            design = design + pltpu.roll(wide, LANES - k * REGRESSORS, 1)
        design = jnp.where(lanes(design.shape) < CONSTANT, design, 0.0)
        part[:, :LANES] = (total[:, :LANES] + design).astype(BF16)
        part[:, LANES:] = total[:, LANES:].astype(BF16)
        start += part.shape[0]


def loss_kernel(rows_ref, thresh_ref, rate_ref, *refs):
    solved_refs, (loss_ref, own_ref, split_ref, total_ref) = refs[:-4], refs[-4:]
    adjoint = joined(solved_refs, 0)
    coeffs = joined(solved_refs, 1)
    thresh = thresh_ref[...]
    rate = rate_ref[...]
    split_ref[...] = three_rows(coeffs)
    total_ref[...] = jnp.zeros(total_ref.shape, F32)

    def losses(here):
        loss = softplus(dot(rows_ref[here], split_ref[...]) - thresh)
        total_ref[...] += jnp.sum(loss.reshape(-1, *total_ref.shape), axis=0)

    each_chunk(rows_ref.shape[0], losses)
    summed = jnp.sum(jnp.sum(total_ref[...] * rate, axis=0, keepdims=True), axis=1, keepdims=True)
    loss_ref[...] = jnp.broadcast_to(
        summed / (rows_ref.shape[0] * coeffs.shape[1]), loss_ref.shape
    )
    own = rows_ref[: own_ref.shape[0]]
    fitted = dot(own, split_ref[...])
    seed = rate * sigmoid(fitted - thresh)
    rest = seed - dot(own, three_rows(adjoint))
    design = dot(rest, coeffs, 1, 1, PRECISE) - dot(fitted, adjoint, 1, 1, PRECISE)
    blank = jnp.zeros((design.shape[0], LANES - REGRESSORS), F32)
    design = jnp.concatenate([design, blank], axis=1)
    own_ref[...] = jnp.where(lanes(design.shape) < CONSTANT, design, 0.0)


def total(refs):
    out = refs[0][...].astype(F32)
    for ref in refs[1:]:
        out = out + ref[...].astype(F32)
    return out


def weight_sum_kernel(*refs):
    refs[-1][...] = total(refs[:-1])


def basis_sum_kernel(own_ref, *refs):
    basis = total(refs[:-1])
    refs[-1][:, :LANES] = basis[:, :LANES] + own_ref[...]
    refs[-1][:, LANES:] = basis[:, LANES:]


def call(kernel, outs, *args, name, flops=0, scratch=(), scalars=0):
    size = sum(a.size * a.dtype.itemsize for a in args) + sum(
        math.prod(s) * jnp.dtype(d).itemsize for s, d in outs
    )
    return pl.pallas_call(
        kernel,
        out_shape=[jax.ShapeDtypeStruct(s, d) for s, d in outs],
        in_specs=[pl.BlockSpec(memory_space=pltpu.SMEM)] * scalars
        + [pl.BlockSpec(memory_space=pltpu.VMEM)] * (len(args) - scalars),
        out_specs=[pl.BlockSpec(memory_space=pltpu.VMEM)] * len(outs),
        scratch_shapes=scratch,
        compiler_params=pltpu.CompilerParams(vmem_limit_bytes=VMEM_BYTES),
        cost_estimate=pl.CostEstimate(flops=int(flops), bytes_accessed=int(size), transcendentals=0),
        name=name,
    )(*args)


def shards(
    path_basis, proxy_weight, notional, set_of, threshold_index, threshold_levels, loss_rate
):
    n = lax.axis_size("paths")
    me = lax.axis_index("paths")
    inner_bits, outer_bits = split_bits(n)
    inner, outer = 1 << len(inner_bits), 1 << len(outer_bits)
    path_rows, features = path_basis.shape
    trade_rows = proxy_weight.shape[0]
    paths_all = path_rows * n
    sets = loss_rate.shape[0]
    quarter = sets // inner
    group_paths, group_trades = inner * path_rows, outer * trade_rows

    def swap(x, mask):
        return lax.ppermute(x, "paths", [(d, d ^ mask) for d in range(n)])

    def masks(bits):
        return [
            sum(((m >> j) & 1) << bit for j, bit in enumerate(bits)) for m in range(1 << len(bits))
        ]

    def after(x, *others):
        return lax.optimization_barrier((x, *others))[0]

    def direct(slots, bits):
        return [swap(x, mask) for x, mask in zip(slots[1:], masks(bits)[1:])]

    def halve(slots, bits):
        slots = [[s] for s in slots]
        for bit in reversed(bits):
            count = len(slots) // 2
            last = None
            for k in reversed(range(count)):
                gone = slots[count + k]
                gone = gone[0] if len(gone) == 1 else sum(g.astype(F32) for g in gone).astype(BF16)
                if last is not None:
                    gone = after(gone, last)
                last = swap(gone, 1 << bit)
                slots[k].append(last)
            slots = slots[:count]
        return slots[0]

    basis = [path_basis]
    weights = [proxy_weight]
    for j, bit in enumerate(outer_bits):
        if j == 1:
            break
        weights = weights + [swap(w, 1 << bit) for w in weights]
    for bit in inner_bits:
        basis = basis + [swap(x, 1 << bit) for x in basis]
    for bit in outer_bits[1:]:
        weights = weights + [swap(w if k else after(w, basis[1]), 1 << bit) for k, w in enumerate(weights)]

    width = max(path_rows, trade_rows)
    lead = path_basis[:, :REGRESSORS].T
    lead = jnp.where(jnp.arange(REGRESSORS)[:, None] == CONSTANT, jnp.ones((), BF16), lead)
    small = jnp.concatenate(
        [
            jnp.pad(lead, ((0, 0), (0, width - path_rows))),
            jnp.pad(notional[None, :], ((0, PAD_ROWS - 1), (0, width - trade_rows))),
        ],
        axis=0,
    )[None]
    for j, bit in enumerate(inner_bits + outer_bits):
        small = jnp.concatenate([small, swap(small, 1 << bit)], axis=0)
        if j == 0:
            small = after(small, basis[1])
        if j == 1:
            small = after(small, weights[1])
    design_group = jnp.concatenate([small[k, :REGRESSORS, :path_rows] for k in range(inner)], axis=1)
    notional_group = small[::inner, REGRESSORS, :trade_rows].reshape(1, group_trades).astype(F32)
    member, thresh, rate = call(
        partial(tables_kernel, masks(outer_bits), inner),
        [((sets, group_trades), BF16), ((1, sets), F32), ((1, sets), F32)],
        me.astype(jnp.int32).reshape(1),
        threshold_levels,
        set_of.reshape(n, 1, trade_rows),
        threshold_index.reshape(inner, 1, quarter),
        loss_rate.reshape(inner, 1, quarter),
        name="tables",
        scalars=2,
    )
    value, *moments = call(
        partial(forward_kernel, inner, outer),
        [((group_paths, group_trades), BF16)] + [((REGRESSORS, quarter), F32)] * inner,
        *basis, *weights, notional_group, design_group, member,
        name="forward",
    )
    moment = sum(direct(moments, inner_bits), moments[0])
    (inverse,) = call(
        partial(inverse_kernel, RIDGE_SCALE * paths_all, path_rows),
        [((REGRESSORS, REGRESSORS), F32)],
        small,
        name="inverse",
    )
    moment = after(moment, inverse)
    moments = [moment] + direct([moment] * outer, outer_bits)
    design_all, design_rows = call(
        partial(design_kernel, path_rows),
        [((REGRESSORS, paths_all), BF16), ((paths_all, LANES), BF16)],
        small,
        name="design",
    )
    (solved,) = call(
        partial(solve_kernel, outer),
        [((2 * REGRESSORS, quarter), F32)],
        inverse, design_all, design_rows, thresh, rate, *moments,
        name="solve",
        scratch=[pltpu.VMEM((LANES, quarter), BF16), pltpu.VMEM((REGRESSORS, quarter), F32)],
    )
    solved = [solved] + direct([solved] * inner, inner_bits)
    (slope,) = call(
        partial(slope_kernel, inner, outer),
        [((group_paths, group_trades), F32)],
        *basis, *weights, notional_group,
        name="slope",
    )
    parts = call(
        partial(backward_kernel, 1.0 / math.sqrt(paths_all), inner, outer),
        [((trade_rows, features), BF16)] * outer + [((path_rows, features), BF16)] * inner,
        member, design_rows, slope, value, *solved, *basis, *weights,
        name="backward",
        scratch=[pltpu.VMEM((group_paths, group_trades), BF16)],
    )
    weight_terms = halve(parts[:outer], outer_bits)
    basis_terms = halve(parts[outer:], inner_bits)
    loss, own_adjoint = call(
        loss_kernel,
        [((8, LANES), F32), ((path_rows, LANES), F32)],
        design_rows, thresh, rate, *solved,
        name="loss",
        scratch=[pltpu.VMEM((LANES, sets), BF16), pltpu.VMEM((8, sets), F32)],
    )
    (weight_adjoint,) = call(
        weight_sum_kernel, [((trade_rows, features), F32)], *weight_terms, name="weight_sum"
    )
    (basis_adjoint,) = call(
        basis_sum_kernel, [((path_rows, features), F32)], own_adjoint, *basis_terms, name="basis_sum"
    )
    return (loss[0, :1], basis_adjoint, weight_adjoint)


def solution(mesh):
    placed = (
        P(("groups", "paths"), None),
        P(("groups", "paths"), None),
        P(("groups", "paths")),
        P("groups"),
        P("groups"),
        P("groups"),
        P("groups"),
    )
    return jax.shard_map(
        shards,
        mesh=mesh,
        in_specs=placed,
        out_specs=(P("groups"), P(("groups", "paths"), None), P(("groups", "paths"), None)),
        check_vma=False,
    )
```

time: 71.4 us -> 61.4 us (0.86)
  waiting for transfers between devices: 37.7 us -> 16.1 us
  starting transfers between devices: 13.6 us -> 27.2 us
  local copies, waits for them, and re-layouts: 3.58 us -> 2.11 us
  Pallas kernels: 15 us -> 14 us
    ppermute x20 -> x25, waiting for transfers between devices: 37.7 us -> 16.1 us  [swap(): return lax.ppermute(x, 'paths', [(d, d ^ mask) for d in range(n)])]
    ppermute x20 -> x25, starting transfers between devices: 13.6 us -> 27.2 us  [swap(): return lax.ppermute(x, 'paths', [(d, d ^ mask) for d in range(n)])]
    pallas_call x8 -> x10, Pallas kernels: 15 us -> 14 us  [call(): pl.pallas_call(kernel, out_shape=[jax.ShapeDtypeStruct(s, d) for s, d in...]
    dynamic_slice x1 -> x0, local copies, waits for them, and re-layouts: 0.78 us -> none  [shards(): set_group.append(lax.dynamic_index_in_dim(set_blocks, me ^ mask, 0))]
    unnamed x16 -> x15, local copies, waits for them, and re-layouts: 1.48 us -> 0.79 us
  transfers between devices with their start and end apart: 20 -> 25, of which waited for: 12 -> 12; matrix products, arithmetic and copies ran while one was open for 3% -> 4% of each run, Pallas kernels for 12% -> 14%
where the time goes in v3:
time: 61.4 us; the launch traced here: 61.2 us
  starting transfers between devices  27.2 us (44%)
  waiting for transfers between devices  16.1 us (26%)
  Pallas kernels  14 us (23%)
  local copies, waits for them, and re-layouts  2.11 us (3%)
  other arithmetic  0.88 us (1%)
  between operations  0.85 us (1%)
    ppermute x25, starting transfers between devices, swap(): return lax.ppermute(x, 'paths', [(d, d ^ mask) for d in range(n)])  27.2 us
    ppermute x25, waiting for transfers between devices, swap(): return lax.ppermute(x, 'paths', [(d, d ^ mask) for d in range(n)])  16.1 us
    pallas_call x10, Pallas kernels, call(): pl.pallas_call(kernel, out_shape=[jax.ShapeDtypeStruct(s, d) for s, d in...  14 us
  transfers between devices with their start and end apart: 25, of which 12 were waited for; matrix products, arithmetic and copies ran while one was open for 4% of the time, Pallas kernels for 14%

profile of v3, /device:TPU:0, one launch (start us, length us, event | category | flops | bytes accessed | tf_op | source)
XLA Modules:
  0.0 61.2 jit_solution(15495714108602062291)
XLA Ops:
  0.6 3.0 %collective-permute-start.1 = (bf16[128,512]{1,0:T(8,128)(2,1)}, bf16[128,512]{1,0:T(8,128)(2,1)S(1)}, u32[]{:S(2)}, u32[]{:S(2)}) collective-permute-start(bf16[128,512]{1,0:T(8,128)(2,1)} %refs_4_.5), channel_id=1, source_target_pairs={{0,2},{1,3},{2,0},{3,1},{4,6},{5,7},{6,4},{7,5},{8,10},{9,11},{10,... | collective-permute-start | bytes 393224 | tf_op jit(solution)/shard_map/ppermute | solution.py:294
  5.3 3.1 %collective-permute-start.3 = (bf16[128,512]{1,0:T(8,128)(2,1)}, bf16[128,512]{1,0:T(8,128)(2,1)S(1)}, u32[]{:S(2)}, u32[]{:S(2)}) collective-permute-start(bf16[128,512]{1,0:T(8,128)(2,1)} %refs_8_.1), channel_id=1, source_target_pairs={{0,8},{1,9},{2,10},{3,11},{4,12},{5,13},{6,14},{7,15},{8,0},{9,1},... | collective-permute-start | bytes 393224 | tf_op jit(solution)/shard_map/ppermute | solution.py:294
  9.0 1.6 %collective-permute-start.2 = (bf16[2,48,128]{2,1,0:T(8,128)(2,1)S(1)}, bf16[2,48,128]{2,1,0:T(8,128)(2,1)S(1)}, u32[]{:S(2)}, u32[]{:S(2)}) collective-permute-start(bf16[2,48,128]{2,1,0:T(8,128)(2,1)S(1)} %pad_maximum_fusion.3), channel_id=1, source_target_pairs={{0,4},{1,5},{2,6},{3,7},{4,0},{5,1},{6,2},{7,3},{8,12},{9,13},{10,... | collective-permute-start | bytes 73736 | tf_op jit(solution)/shard_map/ppermute | solution.py:294
  12.6 1.6 %collective-permute-start.7 = (bf16[128,512]{1,0:T(8,128)(2,1)S(1)}, bf16[128,512]{1,0:T(8,128)(2,1)S(1)}, u32[]{:S(2)}, u32[]{:S(2)}) collective-permute-start(bf16[128,512]{1,0:T(8,128)(2,1)S(1)} %collective-permute-done.1.refs_1_.refs_5_), channel_id=1, source_target_pairs={{0,4},{1,5},{2,6},{3,7},{4,0},{5,1},{6,2},{7,3},{8,12},{9,13},{10,... | collective-permute-start | bytes 393224 | tf_op jit(solution)/shard_map/ppermute | solution.py:294
  14.6 2.5 %collective-permute-start.4 = (bf16[4,48,128]{2,1,0:T(8,128)(2,1)S(1)}, bf16[4,48,128]{2,1,0:T(8,128)(2,1)S(1)}, u32[]{:S(2)}, u32[]{:S(2)}) collective-permute-start(bf16[4,48,128]{2,1,0:T(8,128)(2,1)S(1)} %pad_maximum_fusion.1), channel_id=1, source_target_pairs={{0,8},{1,9},{2,10},{3,11},{4,12},{5,13},{6,14},{7,15},{8,0},{9,1},... | collective-permute-start | bytes 147464 | tf_op jit(solution)/shard_map/ppermute | solution.py:294
  17.1 2.6 %collective-permute-done.4 = bf16[4,48,128]{2,1,0:T(8,128)(2,1)S(1)} collective-permute-done((bf16[4,48,128]{2,1,0:T(8,128)(2,1)S(1)}, bf16[4,48,128]{2,1,0:T(8,128)(2,1)S(1)}, u32[]{:S(2)}, u32[]{:S(2)}) %collective-permute-start.4) | collective-permute-done | bytes 49184 | tf_op jit(solution)/shard_map/ppermute | solution.py:294
  19.8 1.3 %collective-permute-done.5 = bf16[8,48,128]{2,1,0:T(8,128)(2,1)S(1)} collective-permute-done((bf16[8,48,128]{2,1,0:T(8,128)(2,1)S(1)}, bf16[8,48,128]{2,1,0:T(8,128)(2,1)S(1)}, u32[]{:S(2)}, u32[]{:S(2)}) %collective-permute-start.5) | collective-permute-done | bytes 98336 | tf_op jit(solution)/shard_map/ppermute | solution.py:294
  21.2 1.3 %forward.1 = (bf16[512,512]{1,0:T(8,128)(2,1)S(1)}, f32[32,128]{1,0:T(8,128)S(1)}, f32[32,128]{1,0:T(8,128)S(1)}, f32[32,128]{1,0:T(8,128)S(1)}, f32[32,128]{1,0:T(8,128)S(1)}) custom-call(bf16[128,512]{1,0:T(8,128)(2,1)S(1)} %copy-done, bf16[128,512]{1,0:T(8,128)(2,1)S(1)} %collective-permute-done.1.refs_1_.refs_5_, ...), custom_call_target="tpu_custom_call" | custom-call | bytes 2197504 | tf_op jit(solution)/shard_map/forward/pallas_call | solution.py:266
  22.5 2.6 %collective-permute-start.10 = (f32[32,128]{1,0:T(8,128)S(1)}, f32[32,128]{1,0:T(8,128)S(1)}, u32[]{:S(2)}, u32[]{:S(2)}) collective-permute-start(f32[32,128]{1,0:T(8,128)S(1)} %get-tuple-element.38), channel_id=1, source_target_pairs={{0,2},{1,3},{2,0},{3,1},{4,6},{5,7},{6,4},{7,5},{8,10},{9,11},{10,... | collective-permute-start | bytes 49160 | tf_op jit(solution)/shard_map/ppermute | solution.py:294
  25.5 1.0 %collective-permute-start.12 = (f32[32,128]{1,0:T(8,128)S(1)}, f32[32,128]{1,0:T(8,128)S(1)}, u32[]{:S(2)}, u32[]{:S(2)}) collective-permute-start(f32[32,128]{1,0:T(8,128)S(1)} %get-tuple-element.40), channel_id=1, source_target_pairs={{0,6},{1,7},{2,4},{3,5},{4,2},{5,3},{6,0},{7,1},{8,14},{9,15},{10,... | collective-permute-start | bytes 49160 | tf_op jit(solution)/shard_map/ppermute | solution.py:294
  26.5 2.9 %inverse.1.inverse_ref = f32[32,32]{1,0:T(8,128)S(1)} custom-call(bf16[16,48,128]{2,1,0:T(8,128)(2,1)S(1)} %constant_dynamic-update-slice_fusion.small_ref), custom_call_target="tpu_custom_call" | custom-call | bytes 200704 | tf_op jit(solution)/shard_map/inverse/pallas_call | solution.py:266
  30.2 2.7 %collective-permute-start.13 = (f32[32,128]{1,0:T(8,128)S(1)}, f32[32,128]{1,0:T(8,128)S(1)}, u32[]{:S(2)}, u32[]{:S(2)}) collective-permute-start(f32[32,128]{1,0:T(8,128)S(1)} %add_add_fusion.refs_0_), channel_id=1, source_target_pairs={{0,8},{1,9},{2,10},{3,11},{4,12},{5,13},{6,14},{7,15},{8,0},{9,1},... | collective-permute-start | bytes 49160 | tf_op jit(solution)/shard_map/ppermute | solution.py:294
  33.8 1.1 %collective-permute-done.13.refs_1_ = f32[32,128]{1,0:T(8,128)S(1)} collective-permute-done((f32[32,128]{1,0:T(8,128)S(1)}, f32[32,128]{1,0:T(8,128)S(1)}, u32[]{:S(2)}, u32[]{:S(2)}) %collective-permute-start.13) | collective-permute-done | bytes 16416 | tf_op jit(solution)/shard_map/ppermute | solution.py:294
  34.8 2.2 %collective-permute-done.15.refs_3_ = f32[32,128]{1,0:T(8,128)S(1)} collective-permute-done((f32[32,128]{1,0:T(8,128)S(1)}, f32[32,128]{1,0:T(8,128)S(1)}, u32[]{:S(2)}, u32[]{:S(2)}) %collective-permute-start.15) | collective-permute-done | bytes 16416 | tf_op jit(solution)/shard_map/ppermute | solution.py:294
  37.0 1.7 %solve.1.refs_0_ = f32[64,128]{1,0:T(8,128)S(1)} custom-call(f32[32,32]{1,0:T(8,128)S(1)} %inverse.1.inverse_ref, bf16[32,2048]{1,0:T(8,128)(2,1)S(1)} %get-tuple-element.34.design_ref, bf16[2048,128]{1,0:T(8,128)(2,1)S(1)} %get-tuple-element.31.rows_ref, f32[1,512]{1,0:T(1,128)S(1)} %get-tuple-element.32.thresh_ref, ...), custom_call_target="tpu_custom_call" | custom-call | bytes 761856 | tf_op jit(solution)/shard_map/solve/pallas_call | solution.py:266
  38.7 1.1 %collective-permute-start.16 = (f32[64,128]{1,0:T(8,128)S(1)}, f32[64,128]{1,0:T(8,128)S(1)}, u32[]{:S(2)}, u32[]{:S(2)}) collective-permute-start(f32[64,128]{1,0:T(8,128)S(1)} %solve.1.refs_0_), channel_id=1, source_target_pairs={{0,2},{1,3},{2,0},{3,1},{4,6},{5,7},{6,4},{7,5},{8,10},{9,11},{10,... | collective-permute-start | bytes 98312 | tf_op jit(solution)/shard_map/ppermute | solution.py:294
  40.6 1.7 %collective-permute-start.18 = (f32[64,128]{1,0:T(8,128)S(1)}, f32[64,128]{1,0:T(8,128)S(1)}, u32[]{:S(2)}, u32[]{:S(2)}) collective-permute-start(f32[64,128]{1,0:T(8,128)S(1)} %solve.1.refs_0_), channel_id=1, source_target_pairs={{0,6},{1,7},{2,4},{3,5},{4,2},{5,3},{6,0},{7,1},{8,14},{9,15},{10,... | collective-permute-start | bytes 98312 | tf_op jit(solution)/shard_map/ppermute | solution.py:294
  42.2 0.9 %slope.1.slope_ref = f32[512,512]{1,0:T(8,128)S(1)} custom-call(bf16[128,512]{1,0:T(8,128)(2,1)S(1)} %copy-done, bf16[128,512]{1,0:T(8,128)(2,1)S(1)} %collective-permute-done.1.refs_1_.refs_5_, bf16[128,512]{1,0:T(8,128)(2,1)S(1)} %collective-permute-done.6.refs_2_.refs_6_, bf16[128,512]{1,0:T(8,128)(2,1)S(1)} %collective-permute-done.7.refs_3_.refs_7_, ...), custom_call_target="tpu_custom_call" | custom-call | bytes 2099200 | tf_op jit(solution)/shard_map/slope/pallas_call | solution.py:266
  43.9 1.5 %collective-permute-done.18.refs_3_ = f32[64,128]{1,0:T(8,128)S(1)} collective-permute-done((f32[64,128]{1,0:T(8,128)S(1)}, f32[64,128]{1,0:T(8,128)S(1)}, u32[]{:S(2)}, u32[]{:S(2)}) %collective-permute-start.18) | collective-permute-done | bytes 32800 | tf_op jit(solution)/shard_map/ppermute | solution.py:294
  45.4 1.4 %backward.1 = (bf16[128,512]{1,0:T(8,128)(2,1)S(1)}, bf16[128,512]{1,0:T(8,128)(2,1)S(1)}, bf16[128,512]{1,0:T(8,128)(2,1)S(1)}, bf16[128,512]{1,0:T(8,128)(2,1)...) custom-call(bf16[512,512]{1,0:T(8,128)(2,1)S(1)} %get-tuple-element., ...), custom_call_target="tpu_custom_call" | custom-call | bytes 4849664 | tf_op jit(solution)/shard_map/backward/pallas_call | solution.py:266
  46.9 1.4 %collective-permute-start.19 = (bf16[128,512]{1,0:T(8,128)(2,1)S(1)}, bf16[128,512]{1,0:T(8,128)(2,1)S(1)}, u32[]{:S(2)}, u32[]{:S(2)}) collective-permute-start(bf16[128,512]{1,0:T(8,128)(2,1)S(1)} %get-tuple-element.47), channel_id=1, source_target_pairs={{0,4},{1,5},{2,6},{3,7},{4,0},{5,1},{6,2},{7,3},{8,12},{9,13},{10,... | collective-permute-start | bytes 393224 | tf_op jit(solution)/shard_map/ppermute | solution.py:294
  49.1 4.6 %collective-permute-done.19 = bf16[128,512]{1,0:T(8,128)(2,1)S(1)} collective-permute-done((bf16[128,512]{1,0:T(8,128)(2,1)S(1)}, bf16[128,512]{1,0:T(8,128)(2,1)S(1)}, u32[]{:S(2)}, u32[]{:S(2)}) %collective-permute-start.19) | collective-permute-done | bytes 131104 | tf_op jit(solution)/shard_map/ppermute | solution.py:294
  53.7 1.4 %collective-permute-start.21 = (bf16[128,512]{1,0:T(8,128)(2,1)S(1)}, bf16[128,512]{1,0:T(8,128)(2,1)S(1)}, u32[]{:S(2)}, u32[]{:S(2)}) collective-permute-start(bf16[128,512]{1,0:T(8,128)(2,1)S(1)} %add_convert_fusion.1), channel_id=1, source_target_pairs={{0,2},{1,3},{2,0},{3,1},{4,6},{5,7},{6,4},{7,5},{8,10},{9,11},{10,... | collective-permute-start | bytes 393224 | tf_op jit(solution)/shard_map/ppermute | solution.py:294
  55.6 3.2 %loss.1 = (f32[8,128]{1,0:T(8,128)S(1)}, f32[128,128]{1,0:T(8,128)S(1)}) custom-call(bf16[2048,128]{1,0:T(8,128)(2,1)S(1)} %get-tuple-element.31.rows_ref, f32[1,512]{1,0:T(1,128)S(1)} %get-tuple-element.32.thresh_ref, f32[1,512]{1,0:T(1,128)S(1)} %get-tuple-element.33.rate_ref, f32[64,128]{1,0:T(8,128)S(1)} %solve.1.refs_0_, ...), custom_call_target="tpu_custom_call" | custom-call | bytes 729088 | tf_op jit(solution)/shard_map/loss/pallas_call | solution.py:266
  (66 shorter events, 11.9 us)
Async XLA Ops:
  0.6 8.4 %collective-permute-start.1 = (bf16[128,512]{1,0:T(8,128)(2,1)}, bf16[128,512]{1,0:T(8,128)(2,1)S(1)}, u32[]{:S(2)}, u32[]{:S(2)}) collective-permute-start(bf16[128,512]{1,0:T(8,128)(2,1)} %refs_4_.5), channel_id=1, source_target_pairs={{0,2},{1,3},{2,0},{3,1},{4,6},{5,7},{6,4},{7,5},{8,10},{9,11},{10,... | collective-permute-start | bytes 393224 | tf_op jit(solution)/shard_map/ppermute | solution.py:294
  5.3 3.7 %collective-permute-start = (bf16[1,48,128]{2,1,0:T(8,128)(2,1)S(1)}, bf16[1,48,128]{2,1,0:T(8,128)(2,1)S(1)}, u32[]{:S(2)}, u32[]{:S(2)}) collective-permute-start(bf16[1,48,128]{2,1,0:T(8,128)(2,1)S(1)} %fusion.2), channel_id=1, source_target_pairs={{0,2},{1,3},{2,0},{3,1},{4,6},{5,7},{6,4},{7,5},{8,10},{9,11},{10,... | collective-permute-start | bytes 36872 | tf_op jit(solution)/shard_map/ppermute | solution.py:294
  5.3 9.1 %collective-permute-start.3 = (bf16[128,512]{1,0:T(8,128)(2,1)}, bf16[128,512]{1,0:T(8,128)(2,1)S(1)}, u32[]{:S(2)}, u32[]{:S(2)}) collective-permute-start(bf16[128,512]{1,0:T(8,128)(2,1)} %refs_8_.1), channel_id=1, source_target_pairs={{0,8},{1,9},{2,10},{3,11},{4,12},{5,13},{6,14},{7,15},{8,0},{9,1},... | collective-permute-start | bytes 393224 | tf_op jit(solution)/shard_map/ppermute | solution.py:294
  9.0 5.5 %collective-permute-start.2 = (bf16[2,48,128]{2,1,0:T(8,128)(2,1)S(1)}, bf16[2,48,128]{2,1,0:T(8,128)(2,1)S(1)}, u32[]{:S(2)}, u32[]{:S(2)}) collective-permute-start(bf16[2,48,128]{2,1,0:T(8,128)(2,1)S(1)} %pad_maximum_fusion.3), channel_id=1, source_target_pairs={{0,4},{1,5},{2,6},{3,7},{4,0},{5,1},{6,2},{7,3},{8,12},{9,13},{10,... | collective-permute-start | bytes 73736 | tf_op jit(solution)/shard_map/ppermute | solution.py:294
  10.7 10.5 %collective-permute-start.6 = (bf16[128,512]{1,0:T(8,128)(2,1)S(1)}, bf16[128,512]{1,0:T(8,128)(2,1)S(1)}, u32[]{:S(2)}, u32[]{:S(2)}) collective-permute-start(bf16[128,512]{1,0:T(8,128)(2,1)S(1)} %copy-done), channel_id=1, source_target_pairs={{0,4},{1,5},{2,6},{3,7},{4,0},{5,1},{6,2},{7,3},{8,12},{9,13},{10,... | collective-permute-start | bytes 393224 | tf_op jit(solution)/shard_map/ppermute | solution.py:294
  12.5 8.6 %collective-permute-start.8 = (bf16[128,512]{1,0:T(8,128)(2,1)}, bf16[128,512]{1,0:T(8,128)(2,1)S(1)}, u32[]{:S(2)}, u32[]{:S(2)}) collective-permute-start(bf16[128,512]{1,0:T(8,128)(2,1)} %refs_8_.1), channel_id=1, source_target_pairs={{0,1},{1,0},{2,3},{3,2},{4,5},{5,4},{6,7},{7,6},{8,9},{9,8},{10,11... | collective-permute-start | bytes 393224 | tf_op jit(solution)/shard_map/ppermute | solution.py:294
  12.6 8.6 %collective-permute-start.7 = (bf16[128,512]{1,0:T(8,128)(2,1)S(1)}, bf16[128,512]{1,0:T(8,128)(2,1)S(1)}, u32[]{:S(2)}, u32[]{:S(2)}) collective-permute-start(bf16[128,512]{1,0:T(8,128)(2,1)S(1)} %collective-permute-done.1.refs_1_.refs_5_), channel_id=1, source_target_pairs={{0,4},{1,5},{2,6},{3,7},{4,0},{5,1},{6,2},{7,3},{8,12},{9,13},{10,... | collective-permute-start | bytes 393224 | tf_op jit(solution)/shard_map/ppermute | solution.py:294
  14.4 6.7 %collective-permute-start.9 = (bf16[128,512]{1,0:T(8,128)(2,1)S(1)}, bf16[128,512]{1,0:T(8,128)(2,1)S(1)}, u32[]{:S(2)}, u32[]{:S(2)}) collective-permute-start(bf16[128,512]{1,0:T(8,128)(2,1)S(1)} %collective-permute-done.3.refs_5_.refs_9_), channel_id=1, source_target_pairs={{0,1},{1,0},{2,3},{3,2},{4,5},{5,4},{6,7},{7,6},{8,9},{9,8},{10,11... | collective-permute-start | bytes 393224 | tf_op jit(solution)/shard_map/ppermute | solution.py:294
  14.6 5.1 %collective-permute-start.4 = (bf16[4,48,128]{2,1,0:T(8,128)(2,1)S(1)}, bf16[4,48,128]{2,1,0:T(8,128)(2,1)S(1)}, u32[]{:S(2)}, u32[]{:S(2)}) collective-permute-start(bf16[4,48,128]{2,1,0:T(8,128)(2,1)S(1)} %pad_maximum_fusion.1), channel_id=1, source_target_pairs={{0,8},{1,9},{2,10},{3,11},{4,12},{5,13},{6,14},{7,15},{8,0},{9,1},... | collective-permute-start | bytes 147464 | tf_op jit(solution)/shard_map/ppermute | solution.py:294
  22.5 6.9 %collective-permute-start.10 = (f32[32,128]{1,0:T(8,128)S(1)}, f32[32,128]{1,0:T(8,128)S(1)}, u32[]{:S(2)}, u32[]{:S(2)}) collective-permute-start(f32[32,128]{1,0:T(8,128)S(1)} %get-tuple-element.38), channel_id=1, source_target_pairs={{0,2},{1,3},{2,0},{3,1},{4,6},{5,7},{6,4},{7,5},{8,10},{9,11},{10,... | collective-permute-start | bytes 49160 | tf_op jit(solution)/shard_map/ppermute | solution.py:294
  25.0 4.4 %collective-permute-start.11 = (f32[32,128]{1,0:T(8,128)S(1)}, f32[32,128]{1,0:T(8,128)S(1)}, u32[]{:S(2)}, u32[]{:S(2)}) collective-permute-start(f32[32,128]{1,0:T(8,128)S(1)} %get-tuple-element.39), channel_id=1, source_target_pairs={{0,4},{1,5},{2,6},{3,7},{4,0},{5,1},{6,2},{7,3},{8,12},{9,13},{10,... | collective-permute-start | bytes 49160 | tf_op jit(solution)/shard_map/ppermute | solution.py:294
  25.5 4.6 %collective-permute-start.12 = (f32[32,128]{1,0:T(8,128)S(1)}, f32[32,128]{1,0:T(8,128)S(1)}, u32[]{:S(2)}, u32[]{:S(2)}) collective-permute-start(f32[32,128]{1,0:T(8,128)S(1)} %get-tuple-element.40), channel_id=1, source_target_pairs={{0,6},{1,7},{2,4},{3,5},{4,2},{5,3},{6,0},{7,1},{8,14},{9,15},{10,... | collective-permute-start | bytes 49160 | tf_op jit(solution)/shard_map/ppermute | solution.py:294
  30.2 4.6 %collective-permute-start.13 = (f32[32,128]{1,0:T(8,128)S(1)}, f32[32,128]{1,0:T(8,128)S(1)}, u32[]{:S(2)}, u32[]{:S(2)}) collective-permute-start(f32[32,128]{1,0:T(8,128)S(1)} %add_add_fusion.refs_0_), channel_id=1, source_target_pairs={{0,8},{1,9},{2,10},{3,11},{4,12},{5,13},{6,14},{7,15},{8,0},{9,1},... | collective-permute-start | bytes 49160 | tf_op jit(solution)/shard_map/ppermute | solution.py:294
  32.9 1.9 %collective-permute-start.14 = (f32[32,128]{1,0:T(8,128)S(1)}, f32[32,128]{1,0:T(8,128)S(1)}, u32[]{:S(2)}, u32[]{:S(2)}) collective-permute-start(f32[32,128]{1,0:T(8,128)S(1)} %add_add_fusion.refs_0_), channel_id=1, source_target_pairs={{0,1},{1,0},{2,3},{3,2},{4,5},{5,4},{6,7},{7,6},{8,9},{9,8},{10,11... | collective-permute-start | bytes 49160 | tf_op jit(solution)/shard_map/ppermute | solution.py:294
  32.9 4.1 %collective-permute-start.15 = (f32[32,128]{1,0:T(8,128)S(1)}, f32[32,128]{1,0:T(8,128)S(1)}, u32[]{:S(2)}, u32[]{:S(2)}) collective-permute-start(f32[32,128]{1,0:T(8,128)S(1)} %add_add_fusion.refs_0_), channel_id=1, source_target_pairs={{0,9},{1,8},{2,11},{3,10},{4,13},{5,12},{6,15},{7,14},{8,1},{9,0},... | collective-permute-start | bytes 49160 | tf_op jit(solution)/shard_map/ppermute | solution.py:294
  38.7 4.4 %collective-permute-start.16 = (f32[64,128]{1,0:T(8,128)S(1)}, f32[64,128]{1,0:T(8,128)S(1)}, u32[]{:S(2)}, u32[]{:S(2)}) collective-permute-start(f32[64,128]{1,0:T(8,128)S(1)} %solve.1.refs_0_), channel_id=1, source_target_pairs={{0,2},{1,3},{2,0},{3,1},{4,6},{5,7},{6,4},{7,5},{8,10},{9,11},{10,... | collective-permute-start | bytes 98312 | tf_op jit(solution)/shard_map/ppermute | solution.py:294
  39.8 4.0 %collective-permute-start.17 = (f32[64,128]{1,0:T(8,128)S(1)}, f32[64,128]{1,0:T(8,128)S(1)}, u32[]{:S(2)}, u32[]{:S(2)}) collective-permute-start(f32[64,128]{1,0:T(8,128)S(1)} %solve.1.refs_0_), channel_id=1, source_target_pairs={{0,4},{1,5},{2,6},{3,7},{4,0},{5,1},{6,2},{7,3},{8,12},{9,13},{10,... | collective-permute-start | bytes 98312 | tf_op jit(solution)/shard_map/ppermute | solution.py:294
  40.6 4.8 %collective-permute-start.18 = (f32[64,128]{1,0:T(8,128)S(1)}, f32[64,128]{1,0:T(8,128)S(1)}, u32[]{:S(2)}, u32[]{:S(2)}) collective-permute-start(f32[64,128]{1,0:T(8,128)S(1)} %solve.1.refs_0_), channel_id=1, source_target_pairs={{0,6},{1,7},{2,4},{3,5},{4,2},{5,3},{6,0},{7,1},{8,14},{9,15},{10,... | collective-permute-start | bytes 98312 | tf_op jit(solution)/shard_map/ppermute | solution.py:294
  46.8 1.4 %collective-permute-start.22 = (bf16[128,512]{1,0:T(8,128)(2,1)S(1)}, bf16[128,512]{1,0:T(8,128)(2,1)S(1)}, u32[]{:S(2)}, u32[]{:S(2)}) collective-permute-start(bf16[128,512]{1,0:T(8,128)(2,1)S(1)} %get-tuple-element.52), channel_id=1, source_target_pairs={{0,1},{1,0},{2,3},{3,2},{4,5},{5,4},{6,7},{7,6},{8,9},{9,8},{10,11... | collective-permute-start | bytes 393224 | tf_op jit(solution)/shard_map/ppermute | solution.py:294
  46.9 6.8 %collective-permute-start.19 = (bf16[128,512]{1,0:T(8,128)(2,1)S(1)}, bf16[128,512]{1,0:T(8,128)(2,1)S(1)}, u32[]{:S(2)}, u32[]{:S(2)}) collective-permute-start(bf16[128,512]{1,0:T(8,128)(2,1)S(1)} %get-tuple-element.47), channel_id=1, source_target_pairs={{0,4},{1,5},{2,6},{3,7},{4,0},{5,1},{6,2},{7,3},{8,12},{9,13},{10,... | collective-permute-start | bytes 393224 | tf_op jit(solution)/shard_map/ppermute | solution.py:294
  48.3 11.0 %collective-permute-start.24 = (bf16[128,512]{1,0:T(8,128)(2,1)S(1)}, bf16[128,512]{1,0:T(8,128)(2,1)S(1)}, u32[]{:S(2)}, u32[]{:S(2)}) collective-permute-start(bf16[128,512]{1,0:T(8,128)(2,1)S(1)} %add_convert_fusion), channel_id=1, source_target_pairs={{0,8},{1,9},{2,10},{3,11},{4,12},{5,13},{6,14},{7,15},{8,0},{9,1},... | collective-permute-start | bytes 393224 | tf_op jit(solution)/shard_map/ppermute | solution.py:294
  49.1 10.2 %collective-permute-start.23 = (bf16[128,512]{1,0:T(8,128)(2,1)S(1)}, bf16[128,512]{1,0:T(8,128)(2,1)S(1)}, u32[]{:S(2)}, u32[]{:S(2)}) collective-permute-start(bf16[128,512]{1,0:T(8,128)(2,1)S(1)} %get-tuple-element.53), channel_id=1, source_target_pairs={{0,1},{1,0},{2,3},{3,2},{4,5},{5,4},{6,7},{7,6},{8,9},{9,8},{10,11... | collective-permute-start | bytes 393224 | tf_op jit(solution)/shard_map/ppermute | solution.py:294
  53.7 6.3 %collective-permute-start.21 = (bf16[128,512]{1,0:T(8,128)(2,1)S(1)}, bf16[128,512]{1,0:T(8,128)(2,1)S(1)}, u32[]{:S(2)}, u32[]{:S(2)}) collective-permute-start(bf16[128,512]{1,0:T(8,128)(2,1)S(1)} %add_convert_fusion.1), channel_id=1, source_target_pairs={{0,2},{1,3},{2,0},{3,1},{4,6},{5,7},{6,4},{7,5},{8,10},{9,11},{10,... | collective-permute-start | bytes 393224 | tf_op jit(solution)/shard_map/ppermute | solution.py:294
  55.2 5.2 %collective-permute-start.20 = (bf16[128,512]{1,0:T(8,128)(2,1)S(1)}, bf16[128,512]{1,0:T(8,128)(2,1)S(1)}, u32[]{:S(2)}, u32[]{:S(2)}) collective-permute-start(bf16[128,512]{1,0:T(8,128)(2,1)S(1)} %get-tuple-element.48), channel_id=1, source_target_pairs={{0,4},{1,5},{2,6},{3,7},{4,0},{5,1},{6,2},{7,3},{8,12},{9,13},{10,... | collective-permute-start | bytes 393224 | tf_op jit(solution)/shard_map/ppermute | solution.py:294
  (7 other events, 17.0 us)
